TPU v7x, 256 devices: a whole 4x4x8 slice. The times are simulated.
256 devices in a mesh: expert: 64 (over x, y_hi, z), dp: 4 (over y_lo, core).
Axes of the slice: x: 4, y: 4 (y_hi: 2, y_lo: 2; y = y_hi * 2 + y_lo), z: 8, core: 2. Of those that a mesh axis runs over, the one named last changes fastest.
Arguments:
- tokens: bfloat16 [131072, 1280], P(('expert', 'dp')), may hold values from -24 to 24
- d_out: bfloat16 [131072, 1280], P(('expert', 'dp')), may hold values from -6 to 6
- slot_outputs: bfloat16 [1024, 8, 1280], P(('expert', 'dp')), may hold values from -6 to 6
- router: bfloat16 [1280, 8], replicated, may hold values from -6 to 6
- w_in: bfloat16 [1280, 40960], P(None, 'expert'), may hold values from -0.15625 to 0.15625
- w_out: bfloat16 [40960, 1280], P('expert'), may hold values from -0.078125 to 0.078125
Outputs:
- d_tokens: bfloat16 [131072, 1280], P(('expert', 'dp'))
- d_router: float32 [1280, 8], P(('expert', 'dp'))
- d_w_in: float32 [1280, 40960], P('dp', 'expert')
- d_w_out: float32 [40960, 1280], P('expert', 'dp')
All inputs are finite; a program needn't handle non-finite values.
Results may differ from a plain program's by a relative error of at most 0.028.
Values may be sent and summed in bfloat16 or wider, within the bound.
A program may use at most 64 MiB of HBM per device.

v0:
```python
import jax
import jax.numpy as jnp
from jax import lax
from jax.sharding import PartitionSpec as P

FF = 5120
GROUP_LEN = 128


def gelu_exact(values):
    return jax.nn.gelu(values, approximate=False)


def expert_forward(rows_in, rows_grad, w_first, w_second):
    hidden_pre = jnp.einsum("rnd,dnh->rnh", rows_in, w_first, preferred_element_type=jnp.float32)
    hidden, pull_back = jax.vjp(gelu_exact, hidden_pre)
    hidden_b = hidden.astype(jnp.bfloat16)
    hidden_grad = jnp.einsum(
        "rnd,nhd->rnh", rows_grad, w_second, preferred_element_type=jnp.float32
    )
    pre_grad = pull_back(hidden_grad)[0].astype(jnp.bfloat16)
    return (hidden_b, pre_grad)


def shards(tokens, d_out, slot_outputs, router, w_in, w_out):
    width = tokens.shape[1]
    experts = router.shape[1]
    groups = tokens.shape[0] // GROUP_LEN
    tok_groups = tokens.reshape(groups, GROUP_LEN, width)
    grad_groups = d_out.reshape(groups, GROUP_LEN, width)
    logits = jnp.einsum("gld,de->gle", tok_groups, router, preferred_element_type=jnp.float32)
    dispatch = jax.nn.softmax(logits, axis=1)
    combine = jax.nn.softmax(logits, axis=2)
    dispatch_b = dispatch.astype(jnp.bfloat16)
    combine_b = combine.astype(jnp.bfloat16)
    slot_in = jnp.einsum(
        "gle,gld->ged", dispatch_b, tok_groups, preferred_element_type=jnp.float32
    ).astype(jnp.bfloat16)
    slot_grad = jnp.einsum(
        "gle,gld->ged", combine_b, grad_groups, preferred_element_type=jnp.float32
    ).astype(jnp.bfloat16)
    devices = lax.axis_size("expert")
    columns = w_in.shape[1]
    local_count = max(1, columns // FF)
    local_hidden = min(columns, FF)
    senders = jnp.arange(devices * local_count, dtype=jnp.int32)
    sender_expert = senders // local_count * columns // FF + senders % local_count
    all_in, all_grad = (
        lax.all_gather(slot_in, "expert", axis=0, tiled=True),
        lax.all_gather(slot_grad, "expert", axis=0, tiled=True),
    )
    first_slot = lax.axis_index("expert") * columns // FF
    rows_in = lax.dynamic_slice_in_dim(all_in, first_slot, local_count, 1)
    rows_grad = lax.dynamic_slice_in_dim(all_grad, first_slot, local_count, 1)
    w_first = w_in.reshape(width, local_count, local_hidden)
    w_second = w_out.reshape(local_count, local_hidden, width)
    replicas = lax.axis_size("dp")
    share = width // replicas
    hidden_b, pre_grad = expert_forward(rows_in, rows_grad, w_first, w_second)
    d_w_in = lax.psum_scatter(
        jnp.einsum("rnd,rnh->dnh", rows_in, pre_grad, preferred_element_type=jnp.float32).reshape(
            share * lax.axis_size("dp"), columns
        ),
        "dp",
        scatter_dimension=0,
        tiled=True,
    )
    out_term = jnp.einsum(
        "rnh,rnd->nhd", hidden_b, rows_grad, preferred_element_type=jnp.float32
    ).reshape(columns, width)
    d_w_out = lax.psum_scatter(out_term, "dp", scatter_dimension=1, tiled=True)
    slot_back = jnp.einsum("rnh,dnh->rnd", pre_grad, w_first, preferred_element_type=jnp.float32)
    returned = lax.all_to_all(slot_back, "expert", split_axis=0, concat_axis=1, tiled=True)
    owner_table = (sender_expert[:, None] == jnp.arange(experts, dtype=jnp.int32)[None, :]).astype(
        jnp.float32
    )
    slot_in_grad = jnp.einsum(
        "gsd,se->ged", returned, owner_table, precision=lax.Precision.HIGHEST
    ).astype(jnp.bfloat16)
    combine_grad = jnp.einsum(
        "gld,ged->gle", grad_groups, slot_outputs, preferred_element_type=jnp.float32
    )
    dispatch_grad = jnp.einsum(
        "gld,ged->gle", tok_groups, slot_in_grad, preferred_element_type=jnp.float32
    )
    score = combine * (combine_grad - jnp.sum(combine * combine_grad, axis=2, keepdims=True))
    score = score + dispatch * (
        dispatch_grad - jnp.sum(dispatch * dispatch_grad, axis=1, keepdims=True)
    )
    score_b = score.astype(jnp.bfloat16)
    direct = jnp.einsum(
        "gle,ged->gld", dispatch_b, slot_in_grad, preferred_element_type=jnp.float32
    )
    through = jnp.einsum("gle,de->gld", score_b, router, preferred_element_type=jnp.float32)
    d_tokens = (direct + through).astype(jnp.bfloat16).reshape(groups * GROUP_LEN, width)
    router_term = jnp.einsum("gld,gle->de", tok_groups, score_b, preferred_element_type=jnp.float32)
    d_router = lax.psum_scatter(router_term, ("expert", "dp"), scatter_dimension=0, tiled=True)
    return (d_tokens, d_router, d_w_in, d_w_out)


def solution(mesh):
    return jax.shard_map(
        shards,
        mesh=mesh,
        in_specs=(
            P(("expert", "dp"), None),
            P(("expert", "dp"), None),
            P(("expert", "dp"), None, None),
            P(),
            P(None, "expert"),
            P("expert", None),
        ),
        out_specs=(
            P(("expert", "dp"), None),
            P(("expert", "dp"), None),
            P("dp", "expert"),
            P("expert", "dp"),
        ),
        check_vma=False,
    )
```

profile of v0, /device:TPU:1, one launch (start us, length us, event | category | flops | bytes accessed | tf_op | source)
XLA Modules:
  0.0 435.4 jit_solution(1454893477145935190)
XLA Ops:
  7.2 0.0 copy-start
  7.2 0.0 copy-start.1
  7.2 0.0 all-gather.3.cloned.1.call-start
  7.2 1.9 fusion.48
  9.1 0.6 fusion.90
  9.8 0.0 copy-done.1
  9.8 1.0 convolution_convert_fusion.2
  10.8 0.0 all-gather.3.cloned.1.call-update
  10.8 0.0 all-gather.5.cloned.1.call-start
  10.9 0.1 fusion.91
  11.0 2.2 convolution_convert_fusion.1
  13.2 0.0 all-gather.5.cloned.1.call-update
  13.3 0.0 reduce-scatter.6.cloned.1.call-start
  13.4 131.3 %all-gather.3.cloned.1.call-done = bf16[256,8,1280]{2,1,0:T(8,128)(2,1)} async-done(((bf16[4,8,1280]{2,1,0:T(8,128)(2,1)}), bf16[256,8,1280]{2,1,0:T(8,128)(2,1)}) %all-gather.3.cloned.1.call-update) | async-done | bytes 5242896 | tf_op jit(solution)/shard_map/all_gather | solution.py:49
  144.7 3.8 constant_dynamic-slice_fusion.2
  148.5 0.0 copy-start.2
  148.5 1.1 copy-done.2
  149.6 0.0 copy-done
  149.6 1.5 fusion.42
  151.1 126.5 %all-gather.5.cloned.1.call-done = bf16[256,8,1280]{2,1,0:T(8,128)(2,1)} async-done(((bf16[4,8,1280]{2,1,0:T(8,128)(2,1)}), bf16[256,8,1280]{2,1,0:T(8,128)(2,1)}) %all-gather.5.cloned.1.call-update) | async-done | bytes 5242896 | tf_op jit(solution)/shard_map/all_gather | solution.py:50
  277.7 0.0 copy-start.5
  277.7 3.9 constant_dynamic-slice_fusion.1
  281.6 0.0 copy-start.4
  281.6 1.0 copy-done.4
  282.6 0.0 copy-done.5
  282.6 3.7 fusion.37
  286.3 0.0 reduce-scatter.6.cloned.1.call-update
  286.4 0.0 reduce-scatter.8.cloned.1.call-start
  286.4 0.0 copy-start.3
  286.4 4.0 fusion.27
  290.4 0.0 copy-done.3
  290.4 2.4 convolution_bitcast_fusion
  292.8 4.6 %copy.29 = f32[1280,640]{1,0:T(8,128)} copy(f32[1280,640]{0,1:T(8,128)} %convolution_bitcast_fusion) | data formatting | bytes 6553600
  297.4 0.0 reduce-scatter.8.cloned.1.call-update
  297.4 0.7 convolution_bitcast_fusion.1
  298.1 2.4 copy.23
  300.5 0.0 copy-start.6
  300.6 8.4 %all-to-all-start = ((f32[256,1,1280]{2,1,0:T(1,128)}), f32[256,1,1280]{2,1,0:T(1,128)}, u32[]{:S(2)}, u32[]{:S(2)}) async-start(f32[256,1,1280]{2,1,0:T(1,128)} %copy.23), calls=%async_computation | async-start | bytes 2621440 | tf_op jit(solution)/shard_map/all_to_all | solution.py:73
  309.0 0.0 copy-done.6
  309.0 1.8 fusion.92
  310.8 27.7 %all-to-all-done = f32[256,1,1280]{2,1,0:T(1,128)} async-done(((f32[256,1,1280]{2,1,0:T(1,128)}), f32[256,1,1280]{2,1,0:T(1,128)}, u32[]{:S(2)}, u32[]{:S(2)}) %all-to-all-start) | async-done | bytes 1310752 | tf_op jit(solution)/shard_map/all_to_all | solution.py:73
  338.5 1.9 fusion.5
  340.5 0.4 convolution_bitcast_fusion.4
  340.9 0.6 fusion.16
  341.5 0.3 convolution_bitcast_fusion.2
  341.8 80.5 %all-reduce = f32[1280,8]{0,1:T(8,128)S(1)} all-reduce(f32[1280,8]{0,1:T(8,128)S(1)} %convolution_bitcast_fusion.2), channel_id=2, replica_groups=mesh['expert'=64,'dp'=4] {'expert','dp'}, use_global_device_ids=true, to_apply=%region_6.7.clone | all-reduce | flops 10240 | bytes 81920
  422.3 0.1 constant_dynamic-slice_fusion
  422.4 0.7 copy.25
  423.0 0.0 copy-start.7
  423.0 2.4 fusion.52
  425.5 0.0 copy-done.7
  425.5 3.4 fusion.4
  428.9 0.0 reduce-scatter.6.cloned.1.call-done
  428.9 0.0 reduce-scatter.8.cloned.1.call-done
  (1 shorter events, 0.0 us)
Async XLA Ops:
  7.2 142.4 %copy-start = (bf16[1280,640]{1,0:T(8,128)(2,1)S(1)}, bf16[1280,640]{1,0:T(8,128)(2,1)}, u32[]{:S(2)}) copy-start(bf16[1280,640]{1,0:T(8,128)(2,1)} %param.10) | copy-start | bytes 4915204
  7.2 2.6 copy-start.1
  7.2 137.5 %all-gather.3.cloned.1.call-start = ((), (), s32[]{:S(2)}) async-start(), calls=%async_computation.3 | async-start | bytes 5324800 | tf_op jit(solution)/shard_map/all_gather | solution.py:49
  10.8 266.8 %all-gather.5.cloned.1.call-start = ((), (), s32[]{:S(2)}) async-start(), calls=%async_computation.4 | async-start | bytes 5324800 | tf_op jit(solution)/shard_map/all_gather | solution.py:50
  13.3 415.6 %reduce-scatter.6.cloned.1.call-start = ((), (), s32[]{:S(2)}) async-start(), calls=%async_computation.5 | async-start | bytes 4096000 | tf_op jit(solution)/shard_map/reduce_scatter | solution.py:71
  148.5 1.1 copy-start.2
  277.7 5.0 %copy-start.5 = (f32[256,640]{1,0:T(8,128)S(1)}, f32[256,640]{1,0:T(8,128)}, u32[]{:S(2)}) copy-start(f32[256,640]{1,0:T(8,128)} %fusion.42) | copy-start | bytes 1966084
  281.6 1.1 copy-start.4
  286.4 142.5 %reduce-scatter.8.cloned.1.call-start = ((), (), s32[]{:S(2)}) async-start(), calls=%async_computation.6 | async-start | bytes 4096000
  286.4 4.0 copy-start.3
  300.5 8.5 %copy-start.6 = (bf16[4,8,1280]{2,1,0:T(8,128)(2,1)S(1)}, bf16[4,8,1280]{2,1,0:T(8,128)(2,1)}, u32[]{:S(2)}) copy-start(bf16[4,8,1280]{2,1,0:T(8,128)(2,1)} %param.8) | copy-start | bytes 245764
  300.6 38.0 %all-to-all-start = ((f32[256,1,1280]{2,1,0:T(1,128)}), f32[256,1,1280]{2,1,0:T(1,128)}, u32[]{:S(2)}, u32[]{:S(2)}) async-start(f32[256,1,1280]{2,1,0:T(1,128)} %copy.23), calls=%async_computation | async-start | bytes 2621440 | tf_op jit(solution)/shard_map/all_to_all | solution.py:73
  423.0 2.4 copy-start.7
Sparse Core Ops, SparseCore 0:
  12.2 132.4 all-gather.2
  148.8 128.7 all-gather.4
  286.5 54.2 reduce-scatter.5
  343.7 42.6 reduce-scatter.7
where the time goes:
time: 436 us; the launch traced here: 435 us
  waiting for transfers between devices  286 us (66%)
  blocking collectives  80.5 us (18%)
  matrix products  27.8 us (6%)
  local copies, waits for them, and re-layouts  17.6 us (4%)
  between operations  13.9 us (3%)
  starting transfers between devices  8.6 us (2%)
    all_gather x1, waiting for transfers between devices, shards(): lax.all_gather(slot_in, 'expert', axis=0, tiled=True)  131 us
    all_gather x1, waiting for transfers between devices, shards(): lax.all_gather(slot_grad, 'expert', axis=0, tiled=True)  127 us
    unnamed x1, blocking collectives  80.5 us
    all_to_all x1, waiting for transfers between devices, shards(): lax.all_to_all(slot_back, 'expert', split_axis=0, concat_axis=1, tiled=True)  27.7 us
  transfers between devices with their start and end apart: 5, of which 3 were waited for; matrix products, arithmetic and copies ran while one was open for 8% of the time, Pallas kernels for 0%

commit v1 on v0

v1 whole, which is shorter than its diff:
```python
import functools

import jax
import jax.numpy as jnp
from jax import lax
from jax.experimental import pallas as pl
from jax.experimental.pallas import tpu as pltpu
from jax.sharding import PartitionSpec as P

MESH = pl.DeviceIdType.MESH
F32 = jnp.float32
BF16 = jnp.bfloat16

D = 1280
HALF = D // 2
E = 8
Z = 8
DP = 4
GROUPS = 4
LEN = 128
TOK = GROUPS * LEN
COLS = 640
ROWS = E * GROUPS
QUARTER = D // DP
RBLOCK = D // E
RSHARE = RBLOCK // (Z * DP)


def nn(a, b):
    return lax.dot_general(a, b, (((1,), (0,)), ((), ())), preferred_element_type=F32)


def nt(a, b):
    return lax.dot_general(a, b, (((1,), (1,)), ((), ())), preferred_element_type=F32)


def tn(a, b):
    return lax.dot_general(a, b, (((0,), (0,)), ((), ())), preferred_element_type=F32)


def iota(shape, dim):
    return lax.broadcasted_iota(jnp.int32, shape, dim)


def one_hot(rows, cols, source):
    row = iota((rows, cols), 0)
    return (iota((rows, cols), 1) == source(row)).astype(F32).astype(BF16)


def bits(value, low, count):
    return lax.bitwise_and(lax.shift_right_logical(value, jnp.full_like(value, low)), jnp.full_like(value, count - 1))


def kernel(
    tok_hbm, dout_hbm, saved_hbm, router_hbm, w1_hbm, w2_hbm,
    dtok_hbm, drouter_ref, dw1_hbm, dw2_hbm,
    tok, dout, saved, router, w1, w2,
    a_send, a_recv, x, hid, pg, own, rs_out, rs_in, ret_out, ret_in,
    dw, dwb, c_in, y_out, y_in, final, dtok,
    r1_out, r1_in, r2_out, r2_in, r3_out, r3_in,
    load_sem, store_sem,
    a_ss, a_rs, g_ss, g_rs, rs_ss, rs_rs, ret_ss, ret_rs,
    c_ss, c_rs, y_ss, y_rs, r1_ss, r1_rs, r2_ss, r2_rs, r3_ss, r3_rs,
):
    expert = lax.axis_index("expert")
    dp = lax.axis_index("dp")
    a = expert // Z
    z = expert % Z
    y_lo = dp // 2
    core = dp % 2

    def at_a(j):
        return lax.rem(a + j, E)

    def at_z(j):
        return lax.rem(z + j, Z)

    def dev_a(j):
        return (at_a(j) * Z + z, dp)

    def dev_z(j):
        return (a * Z + at_z(j), dp)

    def dev_dp(j):
        return (expert, lax.rem(dp + j, DP))

    other_core = (expert, y_lo * 2 + (1 - core))
    other_y = (expert, (1 - y_lo) * 2 + core)

    def send(src, dst, ss, rs, device):
        copy = pltpu.make_async_remote_copy(
            src_ref=src, dst_ref=dst, send_sem=ss, recv_sem=rs, device_id=device, device_id_type=MESH
        )
        copy.start()
        return copy

    loads = []
    for i, (src, dst) in enumerate(
        ((tok_hbm, tok), (router_hbm, router), (dout_hbm, dout), (saved_hbm, saved), (w1_hbm, w1), (w2_hbm, w2))
    ):
        load = pltpu.make_async_copy(src, dst, load_sem.at[i])
        load.start()
        loads.append(load)
    barrier = pltpu.get_barrier_semaphore()
    for j in range(1, E):
        pl.semaphore_signal(barrier, inc=1, device_id=dev_a(j), device_id_type=MESH)
    for j in range(1, Z):
        pl.semaphore_signal(barrier, inc=1, device_id=dev_z(j), device_id_type=MESH)
    for j in range(1, DP):
        pl.semaphore_signal(barrier, inc=1, device_id=dev_dp(j), device_id_type=MESH)

    loads[0].wait()
    loads[1].wait()
    eye = one_hot(E, E, lambda r: r)
    router_t = nt(eye, router[...]).astype(BF16)
    logits = nt(router_t, tok[...])
    parts = []
    for g in range(GROUPS):
        part = logits[:, g * LEN : (g + 1) * LEN]
        part = jnp.exp(part - jnp.max(part, axis=1, keepdims=True))
        parts.append(part / jnp.sum(part, axis=1, keepdims=True))
    dispatch = jnp.concatenate(parts, axis=1)
    combine = jnp.exp(logits - jnp.max(logits, axis=0, keepdims=True))
    combine = combine / jnp.sum(combine, axis=0, keepdims=True)
    dispatch_b = dispatch.astype(BF16)
    combine_b = combine.astype(BF16)

    spread = one_hot(E * 8, E, lambda r: bits(r, 3, E))
    slot = bits(iota((E * 8, TOK), 0), 0, 8)
    group = bits(iota((E * 8, TOK), 1), 7, GROUPS)
    pick_in = jnp.where(slot == group, nn(spread, dispatch_b), 0.0).astype(BF16)
    pick_grad = jnp.where(slot == group + GROUPS, nn(spread, combine_b), 0.0).astype(BF16)
    slots = nn(pick_in, tok[...])
    loads[2].wait()
    slots = (slots + nn(pick_grad, dout[...])).reshape(E, 8, D)
    a_send[...] = jnp.concatenate([slots[:, :, :HALF], slots[:, :, HALF:]], axis=1).astype(BF16)

    pl.semaphore_wait(barrier, E + Z + DP - 3)
    a_copies = []
    for j in range(1, E):
        a_copies.append(
            send(a_send.at[at_a(j)], a_recv.at[a], a_ss.at[j - 1], a_rs.at[j - 1], dev_a(j))
        )
    a_recv[a] = a_send[a]

    loads[3].wait()
    combine_grad = jnp.concatenate(
        [nt(saved[g], dout[g * LEN : (g + 1) * LEN, :]) for g in range(GROUPS)], axis=1
    )
    score_combine = combine * (combine_grad - jnp.sum(combine * combine_grad, axis=0, keepdims=True))

    order = one_hot(
        4 * ROWS, 4 * ROWS, lambda r: bits(r, 2, 8) * 16 + bits(r, 5, 2) * 8 + bits(r, 6, 2) * 4 + bits(r, 0, 4)
    )
    for copy in a_copies:
        copy.wait_recv()
    chunk = nn(order, a_recv[...].reshape(4 * ROWS, HALF)).astype(BF16)
    for k in range(2):
        x[k, z, :, :HALF] = chunk[2 * k * ROWS : (2 * k + 1) * ROWS]
        x[k, z, :, HALF:] = chunk[(2 * k + 1) * ROWS : (2 * k + 2) * ROWS]

    hops = {}

    def hop(way, r, k):
        step = 1 if way == 0 else Z - 1
        held = at_z((Z - step) * (r - 1) % Z)
        hops[way, r, k] = send(
            x.at[k, held], x.at[k, held], g_ss.at[way, k, r - 1], g_rs.at[way, k, r - 1], dev_z(step)
        )

    rs_copies = {}

    def expert_rows(offsets):
        chunks = [at_z(d) for d in offsets]
        x_in = jnp.concatenate([x[0, c] for c in chunks], axis=0)
        x_grad = jnp.concatenate([x[1, c] for c in chunks], axis=0)
        pre = nn(x_in, w1[...])
        hidden_grad = nt(x_grad, w2[...])
        cdf = 0.5 * (1.0 + lax.erf(pre * 0.7071067811865476))
        slope = cdf + pre * jnp.exp(-0.5 * pre * pre) * 0.3989422804014327
        hidden = (pre * cdf).astype(BF16)
        pre_grad = (hidden_grad * slope).astype(BF16)
        back = nt(pre_grad, w1[...])
        for i, (d, c) in enumerate(zip(offsets, chunks)):
            rows = slice(i * ROWS, (i + 1) * ROWS)
            hid[c] = hidden[rows]
            pg[c] = pre_grad[rows]
            if d == 0:
                own[...] = back[rows]
            else:
                rs_out[c] = back[rows].astype(BF16)
                rs_copies[d] = send(
                    rs_out.at[c], rs_in.at[z], rs_ss.at[d - 1], rs_rs.at[d - 1], dev_z(d)
                )

    for k in range(2):
        for way in range(2):
            hop(way, 1, k)
    loads[4].wait()
    loads[5].wait()
    for r in range(1, 4):
        for k in range(2):
            for way in range(2):
                hops[way, r, k].wait_recv()
                if r < 3 or way == k:
                    hop(way, r + 1, k)
        expert_rows(([0] if r == 1 else []) + [Z - r, r])
    hops[0, 4, 0].wait_recv()
    hops[1, 4, 1].wait_recv()
    expert_rows([4])

    grads = (pg[...].reshape(Z * ROWS, COLS), hid[...].reshape(Z * ROWS, COLS))
    for k in range(2):
        for b in range(D // 256):
            block = tn(x[k, :, :, b * 256 : (b + 1) * 256].reshape(Z * ROWS, 256), grads[k])
            dw[k, b * 256 : (b + 1) * 256, :] = block
            dwb[k, b * 256 : (b + 1) * 256, :] = block.astype(BF16)

    def quarter(yl, c):
        return pl.ds(pl.multiple_of((yl * 2 + c) * QUARTER, QUARTER), QUARTER)

    c_copies = {}
    for i, yl in enumerate((1 - y_lo, y_lo)):
        for k in range(2):
            c_copies[i, k] = send(
                dwb.at[k, quarter(yl, 1 - core), :], c_in.at[i, k], c_ss.at[i, k], c_rs.at[i, k], other_core
            )
    y_copies = []
    for k in range(2):
        c_copies[0, k].wait_recv()
        y_out[k] = (dw[k, quarter(1 - y_lo, core), :] + c_in[0, k].astype(F32)).astype(BF16)
        y_copies.append(send(y_out.at[k], y_in.at[k], y_ss.at[k], y_rs.at[k], other_y))

    total = own[...]
    for d in (1, 7, 2, 6, 3, 5, 4):
        rs_copies[d].wait_recv()
        total = total + rs_in[at_z(Z - d)].astype(F32)
    total = total.astype(BF16)
    order = one_hot(2 * ROWS, 2 * ROWS, lambda r: bits(r, 2, 2) * ROWS + bits(r, 3, 8) * 4 + bits(r, 0, 4))
    stacked = jnp.concatenate([total[:, :HALF], total[:, HALF:]], axis=0)
    ret_out[...] = nn(order, stacked).reshape(E, 8, HALF)
    ret_copies = []
    for j in range(1, E):
        ret_copies.append(
            send(ret_out.at[at_a(j)], ret_in.at[a], ret_ss.at[j - 1], ret_rs.at[j - 1], dev_a(j))
        )
    ret_in[a] = ret_out[a]
    order = one_hot(2 * ROWS, 2 * ROWS, lambda r: bits(r, 0, 8) * 8 + bits(r, 5, 2) * 4 + bits(r, 3, 4))
    for copy in ret_copies:
        copy.wait_recv()
    mixed = nn(order, ret_in[...].reshape(2 * ROWS, HALF).astype(BF16))
    slot_grads = jnp.concatenate([mixed[:ROWS], mixed[ROWS:]], axis=1)

    parts = []
    for g in range(GROUPS):
        here = slice(g * LEN, (g + 1) * LEN)
        grad = nt(slot_grads[g * E : (g + 1) * E].astype(BF16), tok[here, :])
        weight = dispatch[:, here]
        parts.append(weight * (grad - jnp.sum(weight * grad, axis=1, keepdims=True)))
    score = (score_combine + jnp.concatenate(parts, axis=1)).astype(BF16)

    router_grad = nn(score, tok[...])
    for b in range(E):
        r1_out[b, :, :RBLOCK] = router_grad[:, b * RBLOCK : (b + 1) * RBLOCK]
        r1_out[b, :, RBLOCK:] = jnp.zeros((E, 256 - RBLOCK), F32)
    r1_copies = []
    for j in range(1, E):
        r1_copies.append(
            send(r1_out.at[at_a(j)], r1_in.at[a], r1_ss.at[j - 1], r1_rs.at[j - 1], dev_a(j))
        )

    stores = []
    router_f = router_t.astype(F32)
    for g in range(GROUPS):
        here = slice(g * LEN, (g + 1) * LEN)
        left = jnp.concatenate([dispatch_b[:, here].astype(F32), score[:, here].astype(F32)], axis=0).astype(BF16)
        right = jnp.concatenate([slot_grads[g * E : (g + 1) * E], router_f], axis=0).astype(BF16)
        dtok[here, :] = tn(left, right).astype(BF16)
        store = pltpu.make_async_copy(dtok.at[here, :], dtok_hbm.at[here, :], store_sem.at[g])
        store.start()
        stores.append(store)

    total = r1_out[a]
    for j, copy in enumerate(r1_copies, 1):
        copy.wait_recv()
        total = total + r1_in[at_a(E - j)]
    r2_out[...] = total
    r2_copies = []
    for j in range(1, Z):
        r2_copies.append(send(r2_out, r2_in.at[z], r2_ss.at[j - 1], r2_rs.at[j - 1], dev_z(j)))

    def finish(k, out):
        c_copies[1, k].wait_recv()
        y_copies[k].wait_recv()
        final[k] = dw[k, quarter(y_lo, core), :] + c_in[1, k].astype(F32) + y_in[k].astype(F32)
        store = pltpu.make_async_copy(final.at[k], out, store_sem.at[GROUPS + k])
        store.start()
        stores.append(store)

    for j, copy in enumerate(r2_copies, 1):
        copy.wait_recv()
        total = total + r2_in[at_z(Z - j)]
    r3_out[...] = total
    r3_copies = []
    for j in range(1, DP):
        r3_copies.append(send(r3_out, r3_in.at[dp], r3_ss.at[j - 1], r3_rs.at[j - 1], dev_dp(j)))
    finish(0, dw1_hbm)
    finish(1, dw2_hbm)
    for j, copy in enumerate(r3_copies, 1):
        copy.wait_recv()
        total = total + r3_in[lax.rem(dp + DP - j, DP)]
    first = (z * DP + dp) * RSHARE
    pick = (iota((E, 256), 1) == first + iota((E, 256), 0)).astype(F32)
    mine = lax.dot_general(
        pick, total, (((1,), (1,)), ((), ())), precision=lax.Precision.HIGHEST, preferred_element_type=F32
    )
    drouter_ref[...] = mine[:RSHARE]

    for store in stores:
        store.wait()
    for copy in (
        a_copies + list(hops.values()) + list(rs_copies.values()) + ret_copies
        + list(c_copies.values()) + y_copies + r1_copies + r2_copies + r3_copies
    ):
        copy.wait_send()


def shards(tokens, d_out, slot_outputs, router, w_in, w_out):
    dma = pltpu.SemaphoreType.DMA
    vmem = pltpu.VMEM
    any_space = pl.BlockSpec(memory_space=pl.ANY)
    d_tokens, d_router, d_w_in, d_w_out_t = pl.pallas_call(
        kernel,
        out_shape=(
            jax.ShapeDtypeStruct((TOK, D), BF16),
            jax.ShapeDtypeStruct((RSHARE, E), F32),
            jax.ShapeDtypeStruct((QUARTER, COLS), F32),
            jax.ShapeDtypeStruct((QUARTER, COLS), F32),
        ),
        in_specs=[any_space] * 6,
        out_specs=(any_space, pl.BlockSpec(memory_space=pltpu.VMEM), any_space, any_space),
        scratch_shapes=[
            vmem((TOK, D), BF16),
            vmem((TOK, D), BF16),
            vmem((GROUPS, E, D), BF16),
            vmem((D, E), BF16),
            vmem((D, COLS), BF16),
            vmem((COLS, D), BF16),
            vmem((E, 16, HALF), BF16),
            vmem((E, 16, HALF), BF16),
            vmem((2, Z, ROWS, D), BF16),
            vmem((Z, ROWS, COLS), BF16),
            vmem((Z, ROWS, COLS), BF16),
            vmem((ROWS, D), F32),
            vmem((Z, ROWS, D), BF16),
            vmem((Z, ROWS, D), BF16),
            vmem((E, 8, HALF), F32),
            vmem((E, 8, HALF), F32),
            vmem((2, D, COLS), F32),
            vmem((2, D, COLS), BF16),
            vmem((2, 2, QUARTER, COLS), BF16),
            vmem((2, QUARTER, COLS), BF16),
            vmem((2, QUARTER, COLS), BF16),
            vmem((2, QUARTER, COLS), F32),
            vmem((TOK, D), BF16),
            vmem((E, E, 256), F32),
            vmem((E, E, 256), F32),
            vmem((E, 256), F32),
            vmem((Z, E, 256), F32),
            vmem((E, 256), F32),
            vmem((DP, E, 256), F32),
            dma((6,)),
            dma((GROUPS + 2,)),
            dma((E - 1,)),
            dma((E - 1,)),
            dma((2, 2, 4)),
            dma((2, 2, 4)),
            dma((Z - 1,)),
            dma((Z - 1,)),
            dma((E - 1,)),
            dma((E - 1,)),
            dma((2, 2)),
            dma((2, 2)),
            dma((2,)),
            dma((2,)),
            dma((E - 1,)),
            dma((E - 1,)),
            dma((Z - 1,)),
            dma((Z - 1,)),
            dma((DP - 1,)),
            dma((DP - 1,)),
        ],
        compiler_params=pltpu.CompilerParams(
            collective_id=0, has_side_effects=True, vmem_limit_bytes=48 * 1024 * 1024
        ),
    )(tokens, d_out, slot_outputs, router, w_in, w_out)
    return (d_tokens, d_router, d_w_in, d_w_out_t.T)


def solution(mesh):
    return jax.shard_map(
        shards,
        mesh=mesh,
        in_specs=(
            P(("expert", "dp"), None),
            P(("expert", "dp"), None),
            P(("expert", "dp"), None, None),
            P(),
            P(None, "expert"),
            P("expert", None),
        ),
        out_specs=(
            P(("expert", "dp"), None),
            P(("expert", "dp"), None),
            P("dp", "expert"),
            P("expert", "dp"),
        ),
        check_vma=False,
    )
```

time: 436 us -> 87.3 us (0.20)
  waiting for transfers between devices: 286 us -> 0 us
  blocking collectives: 80.5 us -> 0 us
  Pallas kernels: 0 us -> 78.5 us
  matrix products: 27.8 us -> 0 us
  between operations: 13.9 us -> 0.66 us
  local copies, waits for them, and re-layouts: 17.6 us -> 7.89 us
  starting transfers between devices: 8.6 us -> 0 us
    all_gather x2 -> x0, waiting for transfers between devices: 258 us -> none  [the longest x1 131 us: shards(): lax.all_gather(slot_in, 'expert', axis=0, tiled=True)]
    unnamed x1 -> x0, blocking collectives: 80.5 us -> none
    pallas_call x0 -> x1, Pallas kernels: none -> 78.5 us  [shards(): pl.pallas_call(kernel, out_shape=(jax.ShapeDtypeStruct((TOK, D), BF16), j...]
    dot_general x14 -> x0, matrix products: 27.8 us -> none  [the longest x1 4 us: expert_forward(): jnp.einsum('rnd,nhd->rnh', rows_grad, w_second, preferred_element_type=jn...]
    all_to_all x1 -> x0, waiting for transfers between devices: 27.7 us -> none  [shards(): lax.all_to_all(slot_back, 'expert', split_axis=0, concat_axis=1, tiled=True)]
    all_to_all x1 -> x0, starting transfers between devices: 8.44 us -> none  [shards(): lax.all_to_all(slot_back, 'expert', split_axis=0, concat_axis=1, tiled=True)]
    dynamic_slice x2 -> x0, local copies, waits for them, and re-layouts: 7.74 us -> none  [the longest x1 3.9 us: shards(): rows_grad = lax.dynamic_slice_in_dim(all_grad, first_slot, local_count, 1)]
  transfers between devices with their start and end apart: 5 -> 0, of which waited for: 3 -> 0; matrix products, arithmetic and copies ran while one was open for 8% -> 0% of each run, Pallas kernels for 0% -> 0%
where the time goes in v1:
time: 87.3 us; the launch traced here: 87 us
  Pallas kernels  78.5 us (90%)
  local copies, waits for them, and re-layouts  7.89 us (9%)
    pallas_call x1, Pallas kernels, shards(): pl.pallas_call(kernel, out_shape=(jax.ShapeDtypeStruct((TOK, D), BF16), j...  78.5 us
    unnamed x11, local copies, waits for them, and re-layouts  7.89 us

profile of v1, /device:TPU:1, one launch (start us, length us, event | category | flops | bytes accessed | tf_op | source)
XLA Modules:
  0.0 87.0 jit_solution(16206674132044389656)
XLA Ops:
  0.6 0.9 %copy.10.router_hbm = bf16[1280,8]{1,0:T(8,128)(2,1)S(1)} copy(bf16[1280,8]{0,1:T(8,128)(2,1)} %param.9) | data formatting | bytes 40960 | tf_op args[3]
  1.6 0.0 copy-start
  1.6 1.3 %copy-done = bf16[512,1280]{1,0:T(8,128)(2,1)S(1)} copy-done((bf16[512,1280]{1,0:T(8,128)(2,1)S(1)}, bf16[512,1280]{1,0:T(8,128)(2,1)}, u32[]{:S(2)}) %copy-start) | copy-done | bytes 1310744
  2.9 0.0 copy-start.1
  2.9 1.3 %copy-done.1 = bf16[512,1280]{1,0:T(8,128)(2,1)S(1)} copy-done((bf16[512,1280]{1,0:T(8,128)(2,1)S(1)}, bf16[512,1280]{1,0:T(8,128)(2,1)}, u32[]{:S(2)}) %copy-start.1) | copy-done | bytes 1310744
  4.2 0.0 copy-start.2
  4.2 0.9 %copy-done.2 = bf16[4,8,1280]{2,1,0:T(8,128)(2,1)S(1)} copy-done((bf16[4,8,1280]{2,1,0:T(8,128)(2,1)S(1)}, bf16[4,8,1280]{2,1,0:T(8,128)(2,1)}, u32[]{:S(2)}) %copy-start.2) | copy-done | bytes 81944
  5.1 78.5 %shard_map.93 = (bf16[512,1280]{1,0:T(8,128)(2,1)S(1)}, f32[5,8]{1,0:T(8,128)S(1)}, f32[320,640]{1,0:T(8,128)S(1)}, f32[320,640]{1,0:T(8,128)S(1)}) custom-call(bf16[512,1280]{1,0:T(8,128)(2,1)S(1)} %copy-done, bf16[512,1280]{1,0:T(8,128)(2,1)S(1)} %copy-done.1, bf16[4,8,1280]{2,1,0:T(8,128)(2,1)S(1)} %copy-done.2, bf16[1280,8]{1,0:T(8,128)(2,1)S(1)} %copy.10.router_hbm, ...), custom_call_target="tpu_custom_call" | custom-call | tf_op jit(solution)/shard_map/pallas_call | solution.py:332
  83.6 1.1 %copy.15 = bf16[512,1280]{1,0:T(8,128)(2,1)} copy(bf16[512,1280]{1,0:T(8,128)(2,1)S(1)} %get-tuple-element.16) | data formatting | bytes 2621440
  84.7 0.6 copy.16
  85.3 0.9 %copy.17 = f32[320,640]{1,0:T(8,128)} copy(f32[320,640]{1,0:T(8,128)S(1)} %get-tuple-element.18) | data formatting | bytes 1638400
  86.1 0.9 %copy.18 = f32[640,320]{0,1:T(8,128)} copy(f32[640,320]{0,1:T(8,128)S(1)} %bitcast.1) | data formatting | bytes 1638400
Async XLA Ops:
  1.6 1.3 %copy-start = (bf16[512,1280]{1,0:T(8,128)(2,1)S(1)}, bf16[512,1280]{1,0:T(8,128)(2,1)}, u32[]{:S(2)}) copy-start(bf16[512,1280]{1,0:T(8,128)(2,1)} %tok_hbm.1) | copy-start | bytes 3932164
  2.9 1.3 %copy-start.1 = (bf16[512,1280]{1,0:T(8,128)(2,1)S(1)}, bf16[512,1280]{1,0:T(8,128)(2,1)}, u32[]{:S(2)}) copy-start(bf16[512,1280]{1,0:T(8,128)(2,1)} %dout_hbm.1) | copy-start | bytes 3932164
  4.2 0.9 %copy-start.2 = (bf16[4,8,1280]{2,1,0:T(8,128)(2,1)S(1)}, bf16[4,8,1280]{2,1,0:T(8,128)(2,1)}, u32[]{:S(2)}) copy-start(bf16[4,8,1280]{2,1,0:T(8,128)(2,1)} %saved_hbm.1) | copy-start | bytes 245764

commit v2 on v1

v2 whole, which is shorter than its diff:
```python
import functools

import jax
import jax.numpy as jnp
from jax import lax
from jax.experimental import pallas as pl
from jax.experimental.pallas import tpu as pltpu
from jax.sharding import PartitionSpec as P

MESH = pl.DeviceIdType.MESH
F32 = jnp.float32
BF16 = jnp.bfloat16

D = 1280
HALF = D // 2
E = 8
Z = 8
DP = 4
GROUPS = 4
LEN = 128
TOK = GROUPS * LEN
BLOCK = 384
COLS = 640
ROWS = E * GROUPS
QUARTER = D // DP
RBLOCK = D // E
RSHARE = RBLOCK // (Z * DP)


def nn(a, b):
    return lax.dot_general(a, b, (((1,), (0,)), ((), ())), preferred_element_type=F32)


def nt(a, b):
    return lax.dot_general(a, b, (((1,), (1,)), ((), ())), preferred_element_type=F32)


def tn(a, b):
    return lax.dot_general(a, b, (((0,), (0,)), ((), ())), preferred_element_type=F32)


def iota(shape, dim):
    return lax.broadcasted_iota(jnp.int32, shape, dim)


def one_hot(rows, cols, source):
    row = iota((rows, cols), 0)
    return (iota((rows, cols), 1) == source(row)).astype(F32).astype(BF16)


def bits(value, low, count):
    return lax.bitwise_and(lax.shift_right_logical(value, jnp.full_like(value, low)), jnp.full_like(value, count - 1))


def kernel(
    tok_hbm, dout_hbm, saved_hbm, router_hbm, w1_hbm, w2_hbm,
    dtok, drouter_ref, dw1_ref, dw2_ref,
    tok, dout, saved, router, w1, w2,
    a_out, a_in, x, hid, pg, back, rs_out, rs_in, ret_out, ret_in,
    dw, dwb, c_in, y_out, y_in,
    r1_out, r1_in, r2_out, r2_in,
    load_sem,
    a_ss, a_rs, g_ss, g_rs, rs_ss, rs_rs, ret_ss, ret_rs,
    c_ss, c_rs, y_ss, y_rs, r1_ss, r1_rs, r2_ss, r2_rs,
):
    expert = lax.axis_index("expert")
    dp = lax.axis_index("dp")
    a = expert // Z
    z = expert % Z
    y_lo = dp // 2
    core = dp % 2

    def at_a(j):
        return lax.rem(a + j, E)

    def at_z(j):
        return lax.rem(z + j, Z)

    def dev_a(j):
        return (at_a(j) * Z + z, dp)

    def dev_z(j):
        return (a * Z + at_z(j), dp)

    shifts = [(i, j) for i in range(E) for j in range(DP) if i or j]
    plane = [(at_a(i) * Z + z, lax.rem(dp + j, DP)) for i, j in shifts]
    other_core = (expert, y_lo * 2 + (1 - core))
    other_y = (expert, (1 - y_lo) * 2 + core)

    def send(src, dst, ss, rs, device):
        copy = pltpu.make_async_remote_copy(
            src_ref=src, dst_ref=dst, send_sem=ss, recv_sem=rs, device_id=device, device_id_type=MESH
        )
        copy.start()
        return copy

    loads = [
        pltpu.make_async_copy(src, dst, load_sem.at[i])
        for i, (src, dst) in enumerate(
            ((tok_hbm, tok), (router_hbm, router), (dout_hbm, dout), (saved_hbm, saved), (w1_hbm, w1), (w2_hbm, w2))
        )
    ]
    loads[0].start()
    loads[1].start()
    barrier = pltpu.get_barrier_semaphore()
    for device in plane + [dev_z(j) for j in range(1, Z)]:
        pl.semaphore_signal(barrier, inc=1, device_id=device, device_id_type=MESH)

    loads[0].wait()
    loads[1].wait()
    for load in loads[2:]:
        load.start()
    logits = nt(router[...], tok[...])
    parts = []
    for g in range(GROUPS):
        part = logits[:, g * LEN : (g + 1) * LEN]
        part = jnp.exp(part - jnp.max(part, axis=1, keepdims=True))
        parts.append(part / jnp.sum(part, axis=1, keepdims=True))
    dispatch = jnp.concatenate(parts, axis=1)
    dispatch_b = dispatch.astype(BF16)
    spread = one_hot(ROWS, E, lambda r: bits(r, 2, E))
    own_group = bits(iota((ROWS, TOK), 0), 0, GROUPS) == bits(iota((ROWS, TOK), 1), 7, GROUPS)
    spread_blocks = [
        jnp.where(bits(iota((E * 16, ROWS), 0), 2, 4) == c, one_hot(E * 16, ROWS, lambda r: bits(r, 4, E) * 4 + bits(r, 0, 4)), 0.0).astype(BF16)
        for c in range(4)
    ]

    def messages(slots):
        slots = jnp.concatenate([slots, jnp.zeros((ROWS, 4 * BLOCK - D), BF16)], axis=1)
        total = nn(spread_blocks[0], slots[:, :BLOCK])
        for c in range(1, 4):
            total = total + nn(spread_blocks[c], slots[:, c * BLOCK : (c + 1) * BLOCK])
        return total.astype(BF16).reshape(E, 16, BLOCK)

    def slot_rows(weights, rows):
        pick = jnp.where(own_group, nn(spread, weights), 0.0).astype(BF16)
        return messages(nn(pick, rows).astype(BF16))

    a_copies = ([], [])

    def dispatch_rows(k):
        for j in range(1, E):
            a_copies[k].append(
                send(a_out.at[k, at_a(j)], a_in.at[k, a], a_ss.at[k, j - 1], a_rs.at[k, j - 1], dev_a(j))
            )
        a_in[k, a] = a_out[k, a]

    a_out[0] = slot_rows(dispatch_b, tok[...])
    pl.semaphore_wait(barrier, E * DP - 1 + Z - 1)
    dispatch_rows(0)
    combine = jnp.exp(logits - jnp.max(logits, axis=0, keepdims=True))
    combine = combine / jnp.sum(combine, axis=0, keepdims=True)
    loads[2].wait()
    a_out[1] = slot_rows(combine.astype(BF16), dout[...])
    dispatch_rows(1)

    order = one_hot(4 * ROWS, 4 * ROWS, lambda r: bits(r, 2, 8) * 16 + bits(r, 5, 4) * 4 + bits(r, 0, 4))
    hops = {}

    def hop(way, r, k, h):
        step = 1 if way == 0 else Z - 1
        held = at_z((Z - step) * (r - 1) % Z)
        hops[way, r, k, h] = send(
            x.at[k, h, held], x.at[k, h, held], g_ss.at[way, r - 1, k, h], g_rs.at[way, r - 1, k, h], dev_z(step)
        )

    for k in range(2):
        for copy in a_copies[k]:
            copy.wait_recv()
        chunk = nn(order, a_in[k].reshape(4 * ROWS, BLOCK)).astype(BF16)
        chunk = jnp.concatenate([chunk[c * ROWS : (c + 1) * ROWS] for c in range(4)], axis=1)
        for h in range(2):
            x[k, h, z] = chunk[:, h * HALF : (h + 1) * HALF]
            for way in range(2):
                hop(way, 1, k, h)

    loads[3].wait()
    combine_grad = jnp.concatenate(
        [nt(saved[g], dout[g * LEN : (g + 1) * LEN, :]) for g in range(GROUPS)], axis=1
    )
    score_combine = combine * (combine_grad - jnp.sum(combine * combine_grad, axis=0, keepdims=True))

    def expert_rows(offsets):
        chunks = [at_z(d) for d in offsets]
        x_in, x_grad = (
            jnp.concatenate([jnp.concatenate([x[k, h, c] for c in chunks], axis=0) for h in range(2)], axis=1)
            for k in range(2)
        )
        pre = nn(x_in, w1[...])
        hidden_grad = nt(x_grad, w2[...])
        cdf = 0.5 * (1.0 + lax.erf(pre * 0.7071067811865476))
        slope = cdf + pre * jnp.exp(-0.5 * pre * pre) * 0.3989422804014327
        hidden = (pre * cdf).astype(BF16)
        pre_grad = (hidden_grad * slope).astype(BF16)
        grads = nt(pre_grad, w1[...])
        for i, c in enumerate(chunks):
            rows = slice(i * ROWS, (i + 1) * ROWS)
            hid[c] = hidden[rows]
            pg[c] = pre_grad[rows]
            back[c] = grads[rows]

    loads[4].wait()
    loads[5].wait()
    for r in range(1, 4):
        for k in range(2):
            for h in range(2):
                for way in range(2):
                    hops[way, r, k, h].wait_recv()
                    if r < 3 or way == k:
                        hop(way, r + 1, k, h)
        expert_rows(([0] if r == 1 else []) + [Z - r, r])
    for k in range(2):
        for h in range(2):
            hops[k, 4, k, h].wait_recv()
    expert_rows([4])

    rs_copies = {}

    def half(h):
        return slice(h * HALF, (h + 1) * HALF)

    def partial(way, d, h):
        step = 1 if way == 0 else Z - 1
        value = back[at_z(step * d % Z), :, half(h)]
        if (way, d + 1, h) in rs_copies:
            rs_copies[way, d + 1, h].wait_recv()
            value = value + rs_in[way, d, h].astype(F32)
        rs_out[way, d - 1, h] = value.astype(BF16)
        rs_copies[way, d, h] = send(
            rs_out.at[way, d - 1, h], rs_in.at[way, d - 1, h], rs_ss.at[way, d - 1, h], rs_rs.at[way, d - 1, h],
            dev_z(step),
        )

    def partials(d, far):
        for way in range(2):
            partial(way, d, way if far else 1 - way)

    partials(4, True)
    partials(3, False)

    grads = (pg[...].reshape(Z * ROWS, COLS), hid[...].reshape(Z * ROWS, COLS))

    def weight_grad(k):
        for h in range(2):
            block = tn(x[k, h].reshape(Z * ROWS, HALF), grads[k])
            dw[k, h * HALF : (h + 1) * HALF, :] = block
            dwb[k, h * HALF : (h + 1) * HALF, :] = block.astype(BF16)

    def quarter(yl, c):
        return pl.ds(pl.multiple_of((yl * 2 + c) * QUARTER, QUARTER), QUARTER)

    c_copies = {}

    def to_core(i, k):
        yl = (1 - y_lo, y_lo)[i]
        c_copies[i, k] = send(
            dwb.at[k, quarter(yl, 1 - core), :], c_in.at[i, k], c_ss.at[i, k], c_rs.at[i, k], other_core
        )

    y_copies = []

    def to_chip(k):
        c_copies[0, k].wait_recv()
        y_out[k] = (dw[k, quarter(1 - y_lo, core), :] + c_in[0, k].astype(F32)).astype(BF16)
        y_copies.append(send(y_out.at[k], y_in.at[k], y_ss.at[k], y_rs.at[k], other_y))

    weight_grad(0)
    to_core(0, 0)
    partials(3, True)
    weight_grad(1)
    to_core(0, 1)
    partials(2, False)
    to_chip(0)
    to_core(1, 0)
    partials(2, True)
    to_core(1, 1)
    partials(1, False)
    partials(1, True)

    halves = []
    for h in range(2):
        value = back[z, :, half(h)]
        for way in range(2):
            rs_copies[way, 1, h].wait_recv()
            value = value + rs_in[way, 0, h].astype(F32)
        halves.append(value.astype(BF16))
    ret_out[...] = messages(jnp.concatenate(halves, axis=1))
    ret_copies = []
    for j in range(1, E):
        ret_copies.append(
            send(ret_out.at[at_a(j)], ret_in.at[a], ret_ss.at[j - 1], ret_rs.at[j - 1], dev_a(j))
        )
    ret_in[a] = ret_out[a]
    order = one_hot(4 * ROWS, 4 * ROWS, lambda r: bits(r, 0, 8) * 16 + bits(r, 5, 4) * 4 + bits(r, 3, 4))
    for copy in ret_copies:
        copy.wait_recv()
    to_chip(1)
    mixed = nn(order, ret_in[...].reshape(4 * ROWS, BLOCK))
    slot_grads = jnp.concatenate([mixed[c * ROWS : (c + 1) * ROWS] for c in range(4)], axis=1)[:, :D]

    parts = []
    for g in range(GROUPS):
        here = slice(g * LEN, (g + 1) * LEN)
        grad = nt(slot_grads[g * E : (g + 1) * E].astype(BF16), tok[here, :])
        weight = dispatch[:, here]
        parts.append(weight * (grad - jnp.sum(weight * grad, axis=1, keepdims=True)))
    score = (score_combine + jnp.concatenate(parts, axis=1)).astype(BF16)

    router_grad = nn(score, tok[...])
    for b in range(E):
        columns = router_grad[:, b * RBLOCK : (b + 1) * RBLOCK]
        columns = jnp.concatenate([columns, jnp.zeros((E, 256 - RBLOCK), F32)], axis=1)
        r1_out[b] = jnp.concatenate([columns[:, :128], columns[:, 128:]], axis=0).astype(BF16)
    r1_copies = []
    for i, device in enumerate(plane):
        r1_copies.append(
            send(r1_out.at[at_a(shifts[i][0])], r1_in.at[a * DP + dp], r1_ss.at[i], r1_rs.at[i], device)
        )

    router_f = router[...].astype(F32)
    for g in range(GROUPS):
        here = slice(g * LEN, (g + 1) * LEN)
        left = jnp.concatenate([dispatch_b[:, here].astype(F32), score[:, here].astype(F32)], axis=0).astype(BF16)
        right = jnp.concatenate([slot_grads[g * E : (g + 1) * E], router_f], axis=0).astype(BF16)
        dtok[here, :] = tn(left, right).astype(BF16)

    total = r1_out[a].astype(F32)
    for (i, j), copy in zip(shifts, r1_copies):
        copy.wait_recv()
        total = total + r1_in[at_a(E - i) * DP + lax.rem(dp + DP - j, DP)].astype(F32)
    r2_out[...] = total.astype(BF16)
    r2_copies = []
    for j in range(1, Z):
        r2_copies.append(send(r2_out, r2_in.at[z], r2_ss.at[j - 1], r2_rs.at[j - 1], dev_z(j)))

    def finish(k, out):
        c_copies[1, k].wait_recv()
        y_copies[k].wait_recv()
        out[...] = dw[k, quarter(y_lo, core), :] + c_in[1, k].astype(F32) + y_in[k].astype(F32)

    finish(0, dw1_ref)
    finish(1, dw2_ref)
    for j, copy in enumerate(r2_copies, 1):
        copy.wait_recv()
        total = total + r2_in[at_z(Z - j)].astype(F32)
    total = jnp.concatenate([total[:E], total[E:]], axis=1)
    first = (z * DP + dp) * RSHARE
    pick = (iota((E, 256), 1) == first + iota((E, 256), 0)).astype(F32)
    mine = lax.dot_general(
        pick, total, (((1,), (1,)), ((), ())), precision=lax.Precision.HIGHEST, preferred_element_type=F32
    )
    drouter_ref[...] = mine[:RSHARE]

    for copy in (
        a_copies[0] + a_copies[1] + list(hops.values()) + list(rs_copies.values()) + ret_copies
        + list(c_copies.values()) + y_copies + r1_copies + r2_copies
    ):
        copy.wait_send()


def deliver(*refs):
    sources, targets, sems = refs[:4], refs[4:8], refs[8]
    copies = [pltpu.make_async_copy(s, t, sems.at[i]) for i, (s, t) in enumerate(zip(sources, targets))]
    for copy in copies:
        copy.start()
    for copy in copies:
        copy.wait()


def shards(tokens, d_out, slot_outputs, router, w_in, w_out):
    dma = pltpu.SemaphoreType.DMA
    vmem = pltpu.VMEM
    outs = (
        jax.ShapeDtypeStruct((TOK, D), BF16),
        jax.ShapeDtypeStruct((RSHARE, E), F32),
        jax.ShapeDtypeStruct((QUARTER, COLS), F32),
        jax.ShapeDtypeStruct((QUARTER, COLS), F32),
    )
    results = pl.pallas_call(
        kernel,
        out_shape=tuple(vmem(o.shape, o.dtype) for o in outs),
        in_specs=[pl.BlockSpec(memory_space=pltpu.HBM)] * 6,
        out_specs=(pl.BlockSpec(memory_space=pltpu.VMEM),) * 4,
        scratch_shapes=[
            vmem((TOK, D), BF16),
            vmem((TOK, D), BF16),
            vmem((GROUPS, E, D), BF16),
            vmem((E, D), BF16),
            vmem((D, COLS), BF16),
            vmem((COLS, D), BF16),
            vmem((2, E, 16, BLOCK), BF16),
            vmem((2, E, 16, BLOCK), BF16),
            vmem((2, 2, Z, ROWS, HALF), BF16),
            vmem((Z, ROWS, COLS), BF16),
            vmem((Z, ROWS, COLS), BF16),
            vmem((Z, ROWS, D), F32),
            vmem((2, 4, 2, ROWS, HALF), BF16),
            vmem((2, 4, 2, ROWS, HALF), BF16),
            vmem((E, 16, BLOCK), BF16),
            vmem((E, 16, BLOCK), BF16),
            vmem((2, D, COLS), F32),
            vmem((2, D, COLS), BF16),
            vmem((2, 2, QUARTER, COLS), BF16),
            vmem((2, QUARTER, COLS), BF16),
            vmem((2, QUARTER, COLS), BF16),
            vmem((E, 16, 128), BF16),
            vmem((E * DP, 16, 128), BF16),
            vmem((16, 128), BF16),
            vmem((Z, 16, 128), BF16),
            dma((6,)),
            dma((2, E - 1)),
            dma((2, E - 1)),
            dma((2, 4, 2, 2)),
            dma((2, 4, 2, 2)),
            dma((2, 4, 2)),
            dma((2, 4, 2)),
            dma((E - 1,)),
            dma((E - 1,)),
            dma((2, 2)),
            dma((2, 2)),
            dma((2,)),
            dma((2,)),
            dma((E * DP - 1,)),
            dma((E * DP - 1,)),
            dma((Z - 1,)),
            dma((Z - 1,)),
        ],
        compiler_params=pltpu.CompilerParams(
            collective_id=0, has_side_effects=True, vmem_limit_bytes=63_900_000
        ),
    )(tokens, d_out, slot_outputs, router.T, w_in, w_out)
    d_tokens, d_router, d_w_in, d_w_out_t = pl.pallas_call(
        deliver,
        out_shape=outs,
        in_specs=[pl.BlockSpec(memory_space=pl.ANY)] * 4,
        out_specs=(pl.BlockSpec(memory_space=pl.ANY),) * 4,
        scratch_shapes=[dma((4,))],
        compiler_params=pltpu.CompilerParams(vmem_limit_bytes=1024 * 1024),
    )(*results)
    return (d_tokens, d_router, d_w_in, d_w_out_t.T)


def solution(mesh):
    return jax.shard_map(
        shards,
        mesh=mesh,
        in_specs=(
            P(("expert", "dp"), None),
            P(("expert", "dp"), None),
            P(("expert", "dp"), None, None),
            P(),
            P(None, "expert"),
            P("expert", None),
        ),
        out_specs=(
            P(("expert", "dp"), None),
            P(("expert", "dp"), None),
            P("dp", "expert"),
            P("expert", "dp"),
        ),
        check_vma=False,
    )
```

time: 87.3 us -> 70.4 us (0.81)
  Pallas kernels: 78.5 us -> 69.6 us
  local copies, waits for them, and re-layouts: 7.89 us -> 0 us
    pallas_call x1 -> x2, Pallas kernels: 78.5 us -> 69.6 us  [the longest x1 68 us: shards(): pl.pallas_call(kernel, out_shape=tuple((vmem(o.shape, o.dtype) for o in o...]
    unnamed x11 -> x0, local copies, waits for them, and re-layouts: 7.89 us -> none
where the time goes in v2:
time: 70.4 us; the launch traced here: 70.3 us
  Pallas kernels  69.6 us (99%)
    pallas_call x1, Pallas kernels, shards(): pl.pallas_call(kernel, out_shape=tuple((vmem(o.shape, o.dtype) for o in o...  68 us
    pallas_call x1, Pallas kernels, shards(): pl.pallas_call(deliver, out_shape=outs, in_specs=[pl.BlockSpec(memory_spa...  1.63 us

profile of v2, /device:TPU:1, one launch (start us, length us, event | category | flops | bytes accessed | tf_op | source)
XLA Modules:
  0.0 70.3 jit_solution(14163548012338429165)
XLA Ops:
  0.6 68.0 %shard_map.93 = (bf16[512,1280]{1,0:T(8,128)(2,1)S(1)}, f32[5,8]{1,0:T(8,128)S(1)}, f32[320,640]{1,0:T(8,128)S(1)}, f32[320,640]{1,0:T(8,128)S(1)}) custom-call(bf16[512,1280]{1,0:T(8,128)(2,1)} %tok_hbm.1, bf16[512,1280]{1,0:T(8,128)(2,1)} %dout_hbm.1, bf16[4,8,1280]{2,1,0:T(8,128)(2,1)} %saved_hbm.1, bf16[8,1280]{1,0:T(8,128)(2,1)} %bitcast.2, ...), custom_call_target="tpu_custom_call" | custom-call | tf_op jit(solution)/shard_map/pallas_call | solution.py:379
  68.6 1.6 %shard_map.94 = (bf16[512,1280]{1,0:T(8,128)(2,1)}, f32[5,8]{1,0:T(8,128)}, f32[320,640]{1,0:T(8,128)}, f32[320,640]{1,0:T(8,128)}) custom-call(bf16[512,1280]{1,0:T(8,128)(2,1)S(1)} %get-tuple-element.12.refs_0_, f32[5,8]{1,0:T(8,128)S(1)} %get-tuple-element.13.refs_1_, f32[320,640]{1,0:T(8,128)S(1)} %get-tuple-element.14.refs_2_, ...), custom_call_target="tpu_custom_call" | custom-call | tf_op jit(solution)/shard_map/pallas_call | solution.py:432

commit v3 on v2

v3 whole, which is shorter than its diff:
```python
import functools

import jax
import jax.numpy as jnp
from jax import lax
from jax.experimental import pallas as pl
from jax.experimental.pallas import tpu as pltpu
from jax.sharding import PartitionSpec as P

MESH = pl.DeviceIdType.MESH
F32 = jnp.float32
BF16 = jnp.bfloat16

D = 1280
HALF = D // 2
E = 8
Z = 8
DP = 4
GROUPS = 4
LEN = 128
TOK = GROUPS * LEN
BLOCK = 384
COLS = 640
ROWS = E * GROUPS
PAIR = 2 * ROWS
QUARTER = D // DP
RBLOCK = D // E
RSHARE = RBLOCK // (Z * DP)


def nn(a, b):
    return lax.dot_general(a, b, (((1,), (0,)), ((), ())), preferred_element_type=F32)


def nt(a, b):
    return lax.dot_general(a, b, (((1,), (1,)), ((), ())), preferred_element_type=F32)


def tn(a, b):
    return lax.dot_general(a, b, (((0,), (0,)), ((), ())), preferred_element_type=F32)


def iota(shape, dim):
    return lax.broadcasted_iota(jnp.int32, shape, dim)


def one_hot(rows, cols, source):
    row = iota((rows, cols), 0)
    return (iota((rows, cols), 1) == source(row)).astype(F32).astype(BF16)


def bits(value, low, count):
    return lax.bitwise_and(lax.shift_right_logical(value, jnp.full_like(value, low)), jnp.full_like(value, count - 1))


def kernel(
    tok_hbm, dout_hbm, saved_hbm, router_hbm, w1_hbm, w2_hbm,
    dtok, drouter_ref, dw1_ref, dw2_ref,
    tok, dout, saved, router, w1, w2,
    a_out, a_in, x, hid, pg, back, rs_out, rs_in, ret_out, ret_in,
    dw, c_out, c_in, y_out, y_in, y_x, y_hid, score_combine,
    r1_out, r1_in, r2_out, r2_in,
    load_sem,
    a_ss, a_rs, g_ss, g_rs, rs_ss, rs_rs, ret_ss, ret_rs,
    c_ss, c_rs, y_ss, y_rs, n_ss, n_rs, r1_ss, r1_rs, r2_ss, r2_rs,
):
    expert = lax.axis_index("expert")
    dp = lax.axis_index("dp")
    a = expert // Z
    z = expert % Z
    y_lo = dp // 2
    core = dp % 2

    def at_a(j):
        return lax.rem(a + j, E)

    def at_z(j):
        return lax.rem(z + j, Z)

    def dev_a(j):
        return (at_a(j) * Z + z, dp)

    def dev_z(j):
        return (a * Z + at_z(j), dp)

    shifts = [(i, j) for i in range(E) for j in range(DP) if i or j]
    plane = [(at_a(i) * Z + z, lax.rem(dp + j, DP)) for i, j in shifts]
    other_core = (expert, y_lo * 2 + (1 - core))
    other_chip = (expert, (1 - y_lo) * 2 + core)

    def worker(j):
        return (at_a(j) * Z + z, y_lo * 2 + 1)

    def remote(src, dst, ss, rs, device):
        return pltpu.make_async_remote_copy(
            src_ref=src, dst_ref=dst, send_sem=ss, recv_sem=rs, device_id=device, device_id_type=MESH
        )

    def send(*args):
        remote(*args).start()

    def arrived(ref, sem):
        remote(ref, ref, sem, sem, other_core).wait_recv()

    def sent(ref, sem):
        remote(ref, ref, sem, sem, other_core).wait_send()

    loads = [
        pltpu.make_async_copy(src, dst, load_sem.at[i])
        for i, (src, dst) in enumerate(
            ((tok_hbm, tok), (router_hbm, router), (dout_hbm, dout), (saved_hbm, saved), (w1_hbm, w1), (w2_hbm, w2))
        )
    ]
    loads[0].start()
    loads[1].start()
    barrier = pltpu.get_barrier_semaphore()
    for device in plane + [dev_z(j) for j in range(1, Z)]:
        pl.semaphore_signal(barrier, inc=1, device_id=device, device_id_type=MESH)

    loads[0].wait()
    loads[1].wait()
    loads[2].start()
    loads[3].start()

    @pl.when(core == 1)
    def _():
        loads[4].start()
        loads[5].start()

    logits = nt(router[...], tok[...])
    parts = []
    for g in range(GROUPS):
        part = logits[:, g * LEN : (g + 1) * LEN]
        part = jnp.exp(part - jnp.max(part, axis=1, keepdims=True))
        parts.append(part / jnp.sum(part, axis=1, keepdims=True))
    dispatch = jnp.concatenate(parts, axis=1)
    dispatch_b = dispatch.astype(BF16)
    spread = one_hot(ROWS, E, lambda r: bits(r, 2, E))
    own_group = bits(iota((ROWS, TOK), 0), 0, GROUPS) == bits(iota((ROWS, TOK), 1), 7, GROUPS)
    spread_blocks = [
        jnp.where(bits(iota((E * 16, ROWS), 0), 2, 4) == c, one_hot(E * 16, ROWS, lambda r: bits(r, 4, E) * 4 + bits(r, 0, 4)), 0.0).astype(BF16)
        for c in range(4)
    ]

    def messages(slots):
        slots = jnp.concatenate([slots, jnp.zeros((ROWS, 4 * BLOCK - D), BF16)], axis=1)
        total = nn(spread_blocks[0], slots[:, :BLOCK])
        for c in range(1, 4):
            total = total + nn(spread_blocks[c], slots[:, c * BLOCK : (c + 1) * BLOCK])
        return total.astype(BF16).reshape(E, 16, BLOCK)

    def slot_rows(weights, rows):
        pick = jnp.where(own_group, nn(spread, weights), 0.0).astype(BF16)
        return messages(nn(pick, rows).astype(BF16))

    def dispatch_rows(k):
        for j in range(1, E):
            send(a_out.at[k, at_a(j)], a_in.at[k, core, a], a_ss.at[k, j], a_rs.at[k, core, j], worker(j))

        @pl.when(core == 0)
        def _():
            send(a_out.at[k, a], a_in.at[k, 0, a], a_ss.at[k, 0], a_rs.at[k, 0, 0], worker(0))

        @pl.when(core == 1)
        def _():
            a_in[k, 1, a] = a_out[k, a]

    a_out[0] = slot_rows(dispatch_b, tok[...])
    pl.semaphore_wait(barrier, E * DP - 1 + Z - 1)
    dispatch_rows(0)
    combine = jnp.exp(logits - jnp.max(logits, axis=0, keepdims=True))
    combine = combine / jnp.sum(combine, axis=0, keepdims=True)
    loads[2].wait()
    a_out[1] = slot_rows(combine.astype(BF16), dout[...])
    dispatch_rows(1)

    def early_score():
        loads[3].wait()
        combine_grad = jnp.concatenate(
            [nt(saved[g], dout[g * LEN : (g + 1) * LEN, :]) for g in range(GROUPS)], axis=1
        )
        score_combine[...] = combine * (combine_grad - jnp.sum(combine * combine_grad, axis=0, keepdims=True))

    def hop(way, r, k, h):
        step = 1 if way == 0 else Z - 1
        held = at_z((Z - step) * (r - 1) % Z)
        send(x.at[k, h, held], x.at[k, h, held], g_ss.at[way, r - 1, k, h], g_rs.at[way, r - 1, k, h], dev_z(step))

    def hop_arrived(way, r, k, h):
        arrived(x.at[k, h, 0], g_rs.at[way, r - 1, k, h])

    def expert_rows(offsets):
        chunks = [at_z(d) for d in offsets]
        for d, c in zip(offsets, chunks):
            send(x.at[1, 1 - y_lo, c], y_x.at[c], n_ss.at[0, d], n_rs.at[0, d], other_chip)
        x_in, x_grad = (
            jnp.concatenate([jnp.concatenate([x[k, h, c] for c in chunks], axis=0) for h in range(2)], axis=1)
            for k in range(2)
        )
        pre = nn(x_in, w1[...])
        hidden_grad = nt(x_grad, w2[...])
        cdf = 0.5 * (1.0 + lax.erf(pre * 0.7071067811865476))
        slope = cdf + pre * jnp.exp(-0.5 * pre * pre) * 0.3989422804014327
        hidden = (pre * cdf).astype(BF16)
        pre_grad = (hidden_grad * slope).astype(BF16)
        grads = nt(pre_grad, w1[...])
        for i, c in enumerate(chunks):
            rows = slice(i * PAIR, (i + 1) * PAIR)
            hid[c] = hidden[rows]
            pg[c] = pre_grad[rows]
            back[c] = grads[rows]
        for d, c in zip(offsets, chunks):
            send(hid.at[c], y_hid.at[c], n_ss.at[1, d], n_rs.at[1, d], other_chip)

    def half(h):
        return slice(h * HALF, (h + 1) * HALF)

    def partial(way, d, h):
        step = 1 if way == 0 else Z - 1
        value = back[at_z(step * d % Z), :, half(h)]
        if d < 3 or (d == 3 and h == way):
            arrived(rs_in.at[way, d, h], rs_rs.at[way, d, h])
            value = value + rs_in[way, d, h].astype(F32)
        rs_out[way, d - 1, h] = value.astype(BF16)
        send(
            rs_out.at[way, d - 1, h], rs_in.at[way, d - 1, h], rs_ss.at[way, d - 1, h], rs_rs.at[way, d - 1, h],
            dev_z(step),
        )

    def partials(d, far):
        for way in range(2):
            partial(way, d, way if far else 1 - way)

    def rows_dot(rows, grads):
        return tn(rows.reshape(Z * PAIR, HALF), grads.reshape(Z * PAIR, COLS))

    def share(k, grad):
        dw[k] = grad[QUARTER:]
        c_out[k] = grad[:QUARTER].astype(BF16)
        send(c_out.at[k], c_in.at[k], c_ss.at[k], c_rs.at[k], other_core)

    def other_in():
        y_out[...] = rows_dot(x[0, 1 - y_lo], pg[...]).astype(BF16).reshape(2, QUARTER, COLS)
        for c in range(2):
            send(y_out.at[c], y_in, y_ss.at[c], y_rs, (expert, (1 - y_lo) * 2 + c))

    def own_in():
        share(0, rows_dot(x[0, y_lo], pg[...]))

    def own_out():
        for d in range(Z):
            arrived(y_x.at[0], n_rs.at[0, d])
            arrived(y_hid.at[0], n_rs.at[1, d])
        share(1, rows_dot(x[1, y_lo], hid[...]) + rows_dot(y_x[...], y_hid[...]))

    @pl.when(core == 0)
    def _():
        early_score()

    @pl.when(core == 1)
    def _():
        order = one_hot(
            4 * PAIR, 4 * PAIR,
            lambda r: bits(r, 5, 2) * 128 + bits(r, 2, 8) * 16 + bits(r, 6, 4) * 4 + bits(r, 0, 4),
        )
        for k in range(2):
            for c in range(2):
                for j in range(c, E):
                    arrived(a_in.at[k, c, 0], a_rs.at[k, c, j])
            chunk = nn(order, a_in[k].reshape(4 * PAIR, BLOCK)).astype(BF16)
            chunk = jnp.concatenate([chunk[b * PAIR : (b + 1) * PAIR] for b in range(4)], axis=1)
            for h in range(2):
                x[k, h, z] = chunk[:, half(h)]
                for way in range(2):
                    hop(way, 1, k, h)
        early_score()
        loads[4].wait()
        loads[5].wait()
        for r in range(1, 4):
            for k in range(2):
                for h in range(2):
                    for way in range(2):
                        hop_arrived(way, r, k, h)
                        if r < 3 or way == k:
                            hop(way, r + 1, k, h)
            expert_rows(([0] if r == 1 else []) + [Z - r, r])
        for k in range(2):
            for h in range(2):
                hop_arrived(k, 4, k, h)
        expert_rows([4])

        partials(4, True)
        partials(3, False)
        other_in()
        partials(3, True)
        partials(2, False)
        own_in()
        partials(2, True)
        own_out()
        partials(1, False)
        partials(1, True)

        halves = []
        for h in range(2):
            value = back[z, :, half(h)]
            for way in range(2):
                arrived(rs_in.at[way, 0, h], rs_rs.at[way, 0, h])
                value = value + rs_in[way, 0, h].astype(F32)
            halves.append(value.astype(BF16))
        total = jnp.concatenate(halves, axis=1)
        for c in range(2):
            ret_out[c] = messages(total[c * ROWS : (c + 1) * ROWS])
            for j in range(c, E):
                send(
                    ret_out.at[c, at_a(j)], ret_in.at[a], ret_ss.at[c, j], ret_rs.at[j],
                    (at_a(j) * Z + z, y_lo * 2 + c),
                )
        ret_in[a] = ret_out[1, a]

    order = one_hot(4 * ROWS, 4 * ROWS, lambda r: bits(r, 0, 8) * 16 + bits(r, 5, 4) * 4 + bits(r, 3, 4))
    for j in range(1, E):
        arrived(ret_in.at[0], ret_rs.at[j])

    @pl.when(core == 0)
    def _():
        arrived(ret_in.at[0], ret_rs.at[0])

    mixed = nn(order, ret_in[...].reshape(4 * ROWS, BLOCK))
    slot_grads = jnp.concatenate([mixed[c * ROWS : (c + 1) * ROWS] for c in range(4)], axis=1)[:, :D]

    parts = []
    for g in range(GROUPS):
        here = slice(g * LEN, (g + 1) * LEN)
        grad = nt(slot_grads[g * E : (g + 1) * E].astype(BF16), tok[here, :])
        weight = dispatch[:, here]
        parts.append(weight * (grad - jnp.sum(weight * grad, axis=1, keepdims=True)))
    score = (score_combine[...] + jnp.concatenate(parts, axis=1)).astype(BF16)

    router_grad = nn(score, tok[...])
    for b in range(E):
        columns = router_grad[:, b * RBLOCK : (b + 1) * RBLOCK]
        columns = jnp.concatenate([columns, jnp.zeros((E, 256 - RBLOCK), F32)], axis=1)
        r1_out[b] = jnp.concatenate([columns[:, :128], columns[:, 128:]], axis=0).astype(BF16)
    for i, device in enumerate(plane):
        send(r1_out.at[at_a(shifts[i][0])], r1_in.at[a * DP + dp], r1_ss.at[i], r1_rs.at[i], device)

    router_f = router[...].astype(F32)
    for g in range(GROUPS):
        here = slice(g * LEN, (g + 1) * LEN)
        left = jnp.concatenate([dispatch_b[:, here].astype(F32), score[:, here].astype(F32)], axis=0).astype(BF16)
        right = jnp.concatenate([slot_grads[g * E : (g + 1) * E], router_f], axis=0).astype(BF16)
        dtok[here, :] = tn(left, right).astype(BF16)

    total = r1_out[a].astype(F32)
    for n, (i, j) in enumerate(shifts):
        arrived(r1_in.at[0], r1_rs.at[n])
        total = total + r1_in[at_a(E - i) * DP + lax.rem(dp + DP - j, DP)].astype(F32)
    r2_out[...] = total.astype(BF16)
    for j in range(1, Z):
        send(r2_out, r2_in.at[z], r2_ss.at[j - 1], r2_rs.at[j - 1], dev_z(j))

    arrived(y_in, y_rs)

    @pl.when(core == 0)
    def _():
        for k in range(2):
            arrived(c_in.at[k], c_rs.at[k])
        dw1_ref[...] = c_in[0].astype(F32) + y_in[...].astype(F32)
        dw2_ref[...] = c_in[1].astype(F32)

    @pl.when(core == 1)
    def _():
        dw1_ref[...] = dw[0] + y_in[...].astype(F32)
        dw2_ref[...] = dw[1]

    for j in range(1, Z):
        arrived(r2_in.at[0], r2_rs.at[j - 1])
        total = total + r2_in[at_z(Z - j)].astype(F32)
    total = jnp.concatenate([total[:E], total[E:]], axis=1)
    first = (z * DP + dp) * RSHARE
    pick = (iota((E, 256), 1) == first + iota((E, 256), 0)).astype(F32)
    mine = lax.dot_general(
        pick, total, (((1,), (1,)), ((), ())), precision=lax.Precision.HIGHEST, preferred_element_type=F32
    )
    drouter_ref[...] = mine[:RSHARE]

    for k in range(2):
        for j in range(1, E):
            sent(a_out.at[k, 0], a_ss.at[k, j])
    for n in range(E * DP - 1):
        sent(r1_out.at[0], r1_ss.at[n])
    for n in range(Z - 1):
        sent(r2_out, r2_ss.at[n])

    @pl.when(core == 0)
    def _():
        for k in range(2):
            sent(a_out.at[k, 0], a_ss.at[k, 0])

    @pl.when(core == 1)
    def _():
        for way in range(2):
            for k in range(2):
                for h in range(2):
                    for r in range(1, 5 if way == k else 4):
                        sent(x.at[k, h, 0], g_ss.at[way, r - 1, k, h])
            for h in range(2):
                for d in range(1, 5 if way == h else 4):
                    sent(rs_out.at[way, d - 1, h], rs_ss.at[way, d - 1, h])
        for k in range(2):
            sent(c_out.at[k], c_ss.at[k])
            sent(y_out.at[k], y_ss.at[k])
            for d in range(Z):
                sent(hid.at[0], n_ss.at[k, d])
        for c in range(2):
            for j in range(c, E):
                sent(ret_out.at[c, 0], ret_ss.at[c, j])


def deliver(*refs):
    sources, targets, sems = refs[:4], refs[4:8], refs[8]
    copies = [pltpu.make_async_copy(s, t, sems.at[i]) for i, (s, t) in enumerate(zip(sources, targets))]
    for copy in copies:
        copy.start()
    for copy in copies:
        copy.wait()


def shards(tokens, d_out, slot_outputs, router, w_in, w_out):
    dma = pltpu.SemaphoreType.DMA
    vmem = pltpu.VMEM
    outs = (
        jax.ShapeDtypeStruct((TOK, D), BF16),
        jax.ShapeDtypeStruct((RSHARE, E), F32),
        jax.ShapeDtypeStruct((QUARTER, COLS), F32),
        jax.ShapeDtypeStruct((QUARTER, COLS), F32),
    )
    results = pl.pallas_call(
        kernel,
        out_shape=tuple(vmem(o.shape, o.dtype) for o in outs),
        in_specs=[pl.BlockSpec(memory_space=pltpu.HBM)] * 6,
        out_specs=(pl.BlockSpec(memory_space=pltpu.VMEM),) * 4,
        scratch_shapes=[
            vmem((TOK, D), BF16),
            vmem((TOK, D), BF16),
            vmem((GROUPS, E, D), BF16),
            vmem((E, D), BF16),
            vmem((D, COLS), BF16),
            vmem((COLS, D), BF16),
            vmem((2, E, 16, BLOCK), BF16),
            vmem((2, 2, E, 16, BLOCK), BF16),
            vmem((2, 2, Z, PAIR, HALF), BF16),
            vmem((Z, PAIR, COLS), BF16),
            vmem((Z, PAIR, COLS), BF16),
            vmem((Z, PAIR, D), F32),
            vmem((2, 4, 2, PAIR, HALF), BF16),
            vmem((2, 4, 2, PAIR, HALF), BF16),
            vmem((2, E, 16, BLOCK), BF16),
            vmem((E, 16, BLOCK), BF16),
            vmem((2, QUARTER, COLS), F32),
            vmem((2, QUARTER, COLS), BF16),
            vmem((2, QUARTER, COLS), BF16),
            vmem((2, QUARTER, COLS), BF16),
            vmem((QUARTER, COLS), BF16),
            vmem((Z, PAIR, HALF), BF16),
            vmem((Z, PAIR, COLS), BF16),
            vmem((E, TOK), F32),
            vmem((E, 16, 128), BF16),
            vmem((E * DP, 16, 128), BF16),
            vmem((16, 128), BF16),
            vmem((Z, 16, 128), BF16),
            dma((6,)),
            dma((2, E)),
            dma((2, 2, E)),
            dma((2, 4, 2, 2)),
            dma((2, 4, 2, 2)),
            dma((2, 4, 2)),
            dma((2, 4, 2)),
            dma((2, E)),
            dma((E,)),
            dma((2,)),
            dma((2,)),
            dma((2,)),
            dma,
            dma((2, Z)),
            dma((2, Z)),
            dma((E * DP - 1,)),
            dma((E * DP - 1,)),
            dma((Z - 1,)),
            dma((Z - 1,)),
        ],
        compiler_params=pltpu.CompilerParams(
            collective_id=0, has_side_effects=True, vmem_limit_bytes=63_900_000
        ),
    )(tokens, d_out, slot_outputs, router.T, w_in, w_out)
    d_tokens, d_router, d_w_in, d_w_out_t = pl.pallas_call(
        deliver,
        out_shape=outs,
        in_specs=[pl.BlockSpec(memory_space=pl.ANY)] * 4,
        out_specs=(pl.BlockSpec(memory_space=pl.ANY),) * 4,
        scratch_shapes=[dma((4,))],
        compiler_params=pltpu.CompilerParams(vmem_limit_bytes=1024 * 1024),
    )(*results)
    return (d_tokens, d_router, d_w_in, d_w_out_t.T)


def solution(mesh):
    return jax.shard_map(
        shards,
        mesh=mesh,
        in_specs=(
            P(("expert", "dp"), None),
            P(("expert", "dp"), None),
            P(("expert", "dp"), None, None),
            P(),
            P(None, "expert"),
            P("expert", None),
        ),
        out_specs=(
            P(("expert", "dp"), None),
            P(("expert", "dp"), None),
            P("dp", "expert"),
            P("expert", "dp"),
        ),
        check_vma=False,
    )
```

time: 70.4 us -> 66 us (0.937)
  Pallas kernels: 69.6 us -> 65.3 us
    pallas_call x1, Pallas kernels: 68 us -> 63.7 us  [shards(): pl.pallas_call(kernel, out_shape=tuple((vmem(o.shape, o.dtype) for o in o...]
where the time goes in v3:
time: 66 us; the launch traced here: 65.9 us
  Pallas kernels  65.3 us (99%)
    pallas_call x1, Pallas kernels, shards(): pl.pallas_call(kernel, out_shape=tuple((vmem(o.shape, o.dtype) for o in o...  63.7 us
    pallas_call x1, Pallas kernels, shards(): pl.pallas_call(deliver, out_shape=outs, in_specs=[pl.BlockSpec(memory_spa...  1.63 us

profile of v3, /device:TPU:1, one launch (start us, length us, event | category | flops | bytes accessed | tf_op | source)
XLA Modules:
  0.0 65.9 jit_solution(923105864536035820)
XLA Ops:
  0.6 63.7 %shard_map.93 = (bf16[512,1280]{1,0:T(8,128)(2,1)S(1)}, f32[5,8]{1,0:T(8,128)S(1)}, f32[320,640]{1,0:T(8,128)S(1)}, f32[320,640]{1,0:T(8,128)S(1)}) custom-call(bf16[512,1280]{1,0:T(8,128)(2,1)} %tok_hbm.1, bf16[512,1280]{1,0:T(8,128)(2,1)} %dout_hbm.1, bf16[4,8,1280]{2,1,0:T(8,128)(2,1)} %saved_hbm.1, bf16[8,1280]{1,0:T(8,128)(2,1)} %bitcast.2, ...), custom_call_target="tpu_custom_call" | custom-call | tf_op jit(solution)/shard_map/pallas_call | solution.py:438
  64.3 1.6 %shard_map.94 = (bf16[512,1280]{1,0:T(8,128)(2,1)}, f32[5,8]{1,0:T(8,128)}, f32[320,640]{1,0:T(8,128)}, f32[320,640]{1,0:T(8,128)}) custom-call(bf16[512,1280]{1,0:T(8,128)(2,1)S(1)} %get-tuple-element.12.refs_0_, f32[5,8]{1,0:T(8,128)S(1)} %get-tuple-element.13.refs_1_, f32[320,640]{1,0:T(8,128)S(1)} %get-tuple-element.14.refs_2_, ...), custom_call_target="tpu_custom_call" | custom-call | tf_op jit(solution)/shard_map/pallas_call | solution.py:496

commit v4 on v3

--- a/solution.py
+++ b/solution.py
@@ -108,31 +108,37 @@
     loads = [
         pltpu.make_async_copy(src, dst, load_sem.at[i])
         for i, (src, dst) in enumerate(
-            ((tok_hbm, tok), (router_hbm, router), (dout_hbm, dout), (saved_hbm, saved), (w1_hbm, w1), (w2_hbm, w2))
+            ((router_hbm, router), (dout_hbm, dout), (saved_hbm, saved), (w1_hbm, w1), (w2_hbm, w2))
         )
     ]
+    groups = [pl.ds(g * LEN, LEN) for g in range(GROUPS)]
+    token_loads = [
+        pltpu.make_async_copy(tok_hbm.at[here, :], tok.at[here, :], load_sem.at[5 + g]) for g, here in enumerate(groups)
+    ]
     loads[0].start()
-    loads[1].start()
+    for load in token_loads:
+        load.start()
     barrier = pltpu.get_barrier_semaphore()
     for device in plane + [dev_z(j) for j in range(1, Z)]:
         pl.semaphore_signal(barrier, inc=1, device_id=device, device_id_type=MESH)
 
     loads[0].wait()
-    loads[1].wait()
+    loads[1].start()
     loads[2].start()
-    loads[3].start()
 
     @pl.when(core == 1)
     def _():
+        loads[3].start()
         loads[4].start()
-        loads[5].start()
-
-    logits = nt(router[...], tok[...])
-    parts = []
-    for g in range(GROUPS):
-        part = logits[:, g * LEN : (g + 1) * LEN]
+
+    logits, parts = [], []
+    for load, here in zip(token_loads, groups):
+        load.wait()
+        logits.append(nt(router[...], tok[here, :]))
+    for part in logits:
         part = jnp.exp(part - jnp.max(part, axis=1, keepdims=True))
         parts.append(part / jnp.sum(part, axis=1, keepdims=True))
+    logits = jnp.concatenate(logits, axis=1)
     dispatch = jnp.concatenate(parts, axis=1)
     dispatch_b = dispatch.astype(BF16)
     spread = one_hot(ROWS, E, lambda r: bits(r, 2, E))
@@ -170,12 +176,12 @@
     dispatch_rows(0)
     combine = jnp.exp(logits - jnp.max(logits, axis=0, keepdims=True))
     combine = combine / jnp.sum(combine, axis=0, keepdims=True)
-    loads[2].wait()
+    loads[1].wait()
     a_out[1] = slot_rows(combine.astype(BF16), dout[...])
     dispatch_rows(1)
 
     def early_score():
-        loads[3].wait()
+        loads[2].wait()
         combine_grad = jnp.concatenate(
             [nt(saved[g], dout[g * LEN : (g + 1) * LEN, :]) for g in range(GROUPS)], axis=1
         )
@@ -218,13 +224,16 @@
     def partial(way, d, h):
         step = 1 if way == 0 else Z - 1
         value = back[at_z(step * d % Z), :, half(h)]
-        if d < 3 or (d == 3 and h == way):
+        if d < 3:
             arrived(rs_in.at[way, d, h], rs_rs.at[way, d, h])
             value = value + rs_in[way, d, h].astype(F32)
+        if d == 1 and h == way:
+            arrived(rs_in.at[way, 3, h], rs_rs.at[way, 3, h])
+            value = value + rs_in[way, 3, h].astype(F32)
         rs_out[way, d - 1, h] = value.astype(BF16)
         send(
             rs_out.at[way, d - 1, h], rs_in.at[way, d - 1, h], rs_ss.at[way, d - 1, h], rs_rs.at[way, d - 1, h],
-            dev_z(step),
+            dev_z(3 * step % Z if d == 4 else step),
         )
 
     def partials(d, far):
@@ -274,8 +283,8 @@
                 for way in range(2):
                     hop(way, 1, k, h)
         early_score()
+        loads[3].wait()
         loads[4].wait()
-        loads[5].wait()
         for r in range(1, 4):
             for k in range(2):
                 for h in range(2):
@@ -284,19 +293,17 @@
                         if r < 3 or way == k:
                             hop(way, r + 1, k, h)
             expert_rows(([0] if r == 1 else []) + [Z - r, r])
+        partials(3, False)
+        partials(3, True)
         for k in range(2):
             for h in range(2):
                 hop_arrived(k, 4, k, h)
         expert_rows([4])
 
         partials(4, True)
-        partials(3, False)
         other_in()
-        partials(3, True)
         partials(2, False)
-        own_in()
         partials(2, True)
-        own_out()
         partials(1, False)
         partials(1, True)
 
@@ -316,6 +323,8 @@
                     (at_a(j) * Z + z, y_lo * 2 + c),
                 )
         ret_in[a] = ret_out[1, a]
+        own_in()
+        own_out()
 
     order = one_hot(4 * ROWS, 4 * ROWS, lambda r: bits(r, 0, 8) * 16 + bits(r, 5, 4) * 4 + bits(r, 3, 4))
     for j in range(1, E):
@@ -351,46 +360,9 @@
         right = jnp.concatenate([slot_grads[g * E : (g + 1) * E], router_f], axis=0).astype(BF16)
         dtok[here, :] = tn(left, right).astype(BF16)
 
-    total = r1_out[a].astype(F32)
-    for n, (i, j) in enumerate(shifts):
-        arrived(r1_in.at[0], r1_rs.at[n])
-        total = total + r1_in[at_a(E - i) * DP + lax.rem(dp + DP - j, DP)].astype(F32)
-    r2_out[...] = total.astype(BF16)
-    for j in range(1, Z):
-        send(r2_out, r2_in.at[z], r2_ss.at[j - 1], r2_rs.at[j - 1], dev_z(j))
-
-    arrived(y_in, y_rs)
-
-    @pl.when(core == 0)
-    def _():
-        for k in range(2):
-            arrived(c_in.at[k], c_rs.at[k])
-        dw1_ref[...] = c_in[0].astype(F32) + y_in[...].astype(F32)
-        dw2_ref[...] = c_in[1].astype(F32)
-
-    @pl.when(core == 1)
-    def _():
-        dw1_ref[...] = dw[0] + y_in[...].astype(F32)
-        dw2_ref[...] = dw[1]
-
-    for j in range(1, Z):
-        arrived(r2_in.at[0], r2_rs.at[j - 1])
-        total = total + r2_in[at_z(Z - j)].astype(F32)
-    total = jnp.concatenate([total[:E], total[E:]], axis=1)
-    first = (z * DP + dp) * RSHARE
-    pick = (iota((E, 256), 1) == first + iota((E, 256), 0)).astype(F32)
-    mine = lax.dot_general(
-        pick, total, (((1,), (1,)), ((), ())), precision=lax.Precision.HIGHEST, preferred_element_type=F32
-    )
-    drouter_ref[...] = mine[:RSHARE]
-
     for k in range(2):
         for j in range(1, E):
             sent(a_out.at[k, 0], a_ss.at[k, j])
-    for n in range(E * DP - 1):
-        sent(r1_out.at[0], r1_ss.at[n])
-    for n in range(Z - 1):
-        sent(r2_out, r2_ss.at[n])
 
     @pl.when(core == 0)
     def _():
@@ -415,6 +387,44 @@
         for c in range(2):
             for j in range(c, E):
                 sent(ret_out.at[c, 0], ret_ss.at[c, j])
+
+    total = r1_out[a].astype(F32)
+    for n, (i, j) in enumerate(shifts):
+        arrived(r1_in.at[0], r1_rs.at[n])
+        total = total + r1_in[at_a(E - i) * DP + lax.rem(dp + DP - j, DP)].astype(F32)
+    r2_out[...] = total.astype(BF16)
+    for j in range(1, Z):
+        send(r2_out, r2_in.at[z], r2_ss.at[j - 1], r2_rs.at[j - 1], dev_z(j))
+
+    for n in range(E * DP - 1):
+        sent(r1_out.at[0], r1_ss.at[n])
+    arrived(y_in, y_rs)
+
+    @pl.when(core == 0)
+    def _():
+        for k in range(2):
+            arrived(c_in.at[k], c_rs.at[k])
+        dw1_ref[...] = c_in[0].astype(F32) + y_in[...].astype(F32)
+        dw2_ref[...] = c_in[1].astype(F32)
+
+    @pl.when(core == 1)
+    def _():
+        dw1_ref[...] = dw[0] + y_in[...].astype(F32)
+        dw2_ref[...] = dw[1]
+
+    for j in range(1, Z):
+        arrived(r2_in.at[0], r2_rs.at[j - 1])
+        total = total + r2_in[at_z(Z - j)].astype(F32)
+    total = jnp.concatenate([total[:E], total[E:]], axis=1)
+    first = (z * DP + dp) * RSHARE
+    pick = (iota((E, 256), 1) == first + iota((E, 256), 0)).astype(F32)
+    mine = lax.dot_general(
+        pick, total, (((1,), (1,)), ((), ())), precision=lax.Precision.HIGHEST, preferred_element_type=F32
+    )
+    drouter_ref[...] = mine[:RSHARE]
+
+    for n in range(Z - 1):
+        sent(r2_out, r2_ss.at[n])
 
 
 def deliver(*refs):
@@ -469,7 +479,7 @@
             vmem((E * DP, 16, 128), BF16),
             vmem((16, 128), BF16),
             vmem((Z, 16, 128), BF16),
-            dma((6,)),
+            dma((5 + GROUPS,)),
             dma((2, E)),
             dma((2, 2, E)),
             dma((2, 4, 2, 2)),

time: 66 us -> 63.2 us (0.958)
  Pallas kernels: 65.3 us -> 62.4 us
    pallas_call x1, Pallas kernels: 63.7 us -> 60.8 us  [shards(): pl.pallas_call(kernel, out_shape=tuple((vmem(o.shape, o.dtype) for o in o...]
where the time goes in v4:
time: 63.2 us; the launch traced here: 63.1 us
  Pallas kernels  62.4 us (99%)
  between operations  0.64 us (1%)
    pallas_call x1, Pallas kernels, shards(): pl.pallas_call(kernel, out_shape=tuple((vmem(o.shape, o.dtype) for o in o...  60.8 us
    pallas_call x1, Pallas kernels, shards(): pl.pallas_call(deliver, out_shape=outs, in_specs=[pl.BlockSpec(memory_spa...  1.63 us

profile of v4, /device:TPU:1, one launch (start us, length us, event | category | flops | bytes accessed | tf_op | source)
XLA Modules:
  0.0 63.1 jit_solution(8865758305824917404)
XLA Ops:
  0.6 60.8 %shard_map.93 = (bf16[512,1280]{1,0:T(8,128)(2,1)S(1)}, f32[5,8]{1,0:T(8,128)S(1)}, f32[320,640]{1,0:T(8,128)S(1)}, f32[320,640]{1,0:T(8,128)S(1)}) custom-call(bf16[512,1280]{1,0:T(8,128)(2,1)} %tok_hbm.1, bf16[512,1280]{1,0:T(8,128)(2,1)} %dout_hbm.1, bf16[4,8,1280]{2,1,0:T(8,128)(2,1)} %saved_hbm.1, bf16[8,1280]{1,0:T(8,128)(2,1)} %bitcast.2, ...), custom_call_target="tpu_custom_call" | custom-call | tf_op jit(solution)/shard_map/pallas_call | solution.py:448
  61.4 1.6 %shard_map.94 = (bf16[512,1280]{1,0:T(8,128)(2,1)}, f32[5,8]{1,0:T(8,128)}, f32[320,640]{1,0:T(8,128)}, f32[320,640]{1,0:T(8,128)}) custom-call(bf16[512,1280]{1,0:T(8,128)(2,1)S(1)} %get-tuple-element.12.refs_0_, f32[5,8]{1,0:T(8,128)S(1)} %get-tuple-element.13.refs_1_, f32[320,640]{1,0:T(8,128)S(1)} %get-tuple-element.14.refs_2_, ...), custom_call_target="tpu_custom_call" | custom-call | tf_op jit(solution)/shard_map/pallas_call | solution.py:506

commit v5 on v4

--- a/solution.py
+++ b/solution.py
@@ -26,6 +26,9 @@
 QUARTER = D // DP
 RBLOCK = D // E
 RSHARE = RBLOCK // (Z * DP)
+FAR_A = (5, 3, 4, 2, 6, 1, 7, 0)
+FAR_Z = (4, 3, 5, 2, 6, 1, 7)
+FAR_DP = (3, 2, 1, 0)
 
 
 def nn(a, b):
@@ -83,7 +86,7 @@
     def dev_z(j):
         return (a * Z + at_z(j), dp)
 
-    shifts = [(i, j) for i in range(E) for j in range(DP) if i or j]
+    shifts = [(i, j) for i in FAR_A for j in FAR_DP if i or j]
     plane = [(at_a(i) * Z + z, lax.rem(dp + j, DP)) for i, j in shifts]
     other_core = (expert, y_lo * 2 + (1 - core))
     other_chip = (expert, (1 - y_lo) * 2 + core)
@@ -160,7 +163,7 @@
         return messages(nn(pick, rows).astype(BF16))
 
     def dispatch_rows(k):
-        for j in range(1, E):
+        for j in FAR_A[:-1]:
             send(a_out.at[k, at_a(j)], a_in.at[k, core, a], a_ss.at[k, j], a_rs.at[k, core, j], worker(j))
 
         @pl.when(core == 0)
@@ -317,7 +320,7 @@
         total = jnp.concatenate(halves, axis=1)
         for c in range(2):
             ret_out[c] = messages(total[c * ROWS : (c + 1) * ROWS])
-            for j in range(c, E):
+            for j in FAR_A[: E - c]:
                 send(
                     ret_out.at[c, at_a(j)], ret_in.at[a], ret_ss.at[c, j], ret_rs.at[j],
                     (at_a(j) * Z + z, y_lo * 2 + c),
@@ -393,7 +396,7 @@
         arrived(r1_in.at[0], r1_rs.at[n])
         total = total + r1_in[at_a(E - i) * DP + lax.rem(dp + DP - j, DP)].astype(F32)
     r2_out[...] = total.astype(BF16)
-    for j in range(1, Z):
+    for j in FAR_Z:
         send(r2_out, r2_in.at[z], r2_ss.at[j - 1], r2_rs.at[j - 1], dev_z(j))
 
     for n in range(E * DP - 1):

time: 63.2 us -> 62.7 us (level)
  no operation moved by 1% of the time
where the time goes in v5:
time: 62.7 us; the launch traced here: 62.6 us
  Pallas kernels  62 us (99%)
  between operations  0.64 us (1%)
    pallas_call x1, Pallas kernels, shards(): pl.pallas_call(kernel, out_shape=tuple((vmem(o.shape, o.dtype) for o in o...  60.4 us
    pallas_call x1, Pallas kernels, shards(): pl.pallas_call(deliver, out_shape=outs, in_specs=[pl.BlockSpec(memory_spa...  1.63 us

profile of v5, /device:TPU:1, one launch (start us, length us, event | category | flops | bytes accessed | tf_op | source)
XLA Modules:
  0.0 62.6 jit_solution(6045210271186593307)
XLA Ops:
  0.6 60.4 %shard_map.93 = (bf16[512,1280]{1,0:T(8,128)(2,1)S(1)}, f32[5,8]{1,0:T(8,128)S(1)}, f32[320,640]{1,0:T(8,128)S(1)}, f32[320,640]{1,0:T(8,128)S(1)}) custom-call(bf16[512,1280]{1,0:T(8,128)(2,1)} %tok_hbm.1, bf16[512,1280]{1,0:T(8,128)(2,1)} %dout_hbm.1, bf16[4,8,1280]{2,1,0:T(8,128)(2,1)} %saved_hbm.1, bf16[8,1280]{1,0:T(8,128)(2,1)} %bitcast.2, ...), custom_call_target="tpu_custom_call" | custom-call | tf_op jit(solution)/shard_map/pallas_call | solution.py:451
  61.0 1.6 %shard_map.94 = (bf16[512,1280]{1,0:T(8,128)(2,1)}, f32[5,8]{1,0:T(8,128)}, f32[320,640]{1,0:T(8,128)}, f32[320,640]{1,0:T(8,128)}) custom-call(bf16[512,1280]{1,0:T(8,128)(2,1)S(1)} %get-tuple-element.12.refs_0_, f32[5,8]{1,0:T(8,128)S(1)} %get-tuple-element.13.refs_1_, f32[320,640]{1,0:T(8,128)S(1)} %get-tuple-element.14.refs_2_, ...), custom_call_target="tpu_custom_call" | custom-call | tf_op jit(solution)/shard_map/pallas_call | solution.py:509

commit v6 on v5

--- a/solution.py
+++ b/solution.py
@@ -122,7 +122,13 @@
     for load in token_loads:
         load.start()
     barrier = pltpu.get_barrier_semaphore()
-    for device in plane + [dev_z(j) for j in range(1, Z)]:
+    greeted = (
+        [dev_a(j) for j in range(1, E)]
+        + [(at_a(j) * Z + z, y_lo * 2 + 1 - core) for j in range(E)]
+        + [dev_z(j) for j in (1, 3, Z - 3, Z - 1)]
+        + [(expert, (1 - y_lo) * 2 + c) for c in range(2)]
+    )
+    for device in greeted:
         pl.semaphore_signal(barrier, inc=1, device_id=device, device_id_type=MESH)
 
     loads[0].wait()
@@ -175,7 +181,7 @@
             a_in[k, 1, a] = a_out[k, a]
 
     a_out[0] = slot_rows(dispatch_b, tok[...])
-    pl.semaphore_wait(barrier, E * DP - 1 + Z - 1)
+    pl.semaphore_wait(barrier, len(greeted))
     dispatch_rows(0)
     combine = jnp.exp(logits - jnp.max(logits, axis=0, keepdims=True))
     combine = combine / jnp.sum(combine, axis=0, keepdims=True)

time: 62.7 us -> 62 us (0.989)
  Pallas kernels: 62 us -> 61.3 us
    pallas_call x1, Pallas kernels: 60.4 us -> 59.7 us  [shards(): pl.pallas_call(kernel, out_shape=tuple((vmem(o.shape, o.dtype) for o in o...]
where the time goes in v6:
time: 62 us; the launch traced here: 61.9 us
  Pallas kernels  61.3 us (99%)
  between operations  0.64 us (1%)
    pallas_call x1, Pallas kernels, shards(): pl.pallas_call(kernel, out_shape=tuple((vmem(o.shape, o.dtype) for o in o...  59.7 us
    pallas_call x1, Pallas kernels, shards(): pl.pallas_call(deliver, out_shape=outs, in_specs=[pl.BlockSpec(memory_spa...  1.63 us

profile of v6, /device:TPU:1, one launch (start us, length us, event | category | flops | bytes accessed | tf_op | source)
XLA Modules:
  0.0 61.9 jit_solution(5627092962109612749)
XLA Ops:
  0.6 59.7 %shard_map.93 = (bf16[512,1280]{1,0:T(8,128)(2,1)S(1)}, f32[5,8]{1,0:T(8,128)S(1)}, f32[320,640]{1,0:T(8,128)S(1)}, f32[320,640]{1,0:T(8,128)S(1)}) custom-call(bf16[512,1280]{1,0:T(8,128)(2,1)} %tok_hbm.1, bf16[512,1280]{1,0:T(8,128)(2,1)} %dout_hbm.1, bf16[4,8,1280]{2,1,0:T(8,128)(2,1)} %saved_hbm.1, bf16[8,1280]{1,0:T(8,128)(2,1)} %bitcast.2, ...), custom_call_target="tpu_custom_call" | custom-call | tf_op jit(solution)/shard_map/pallas_call | solution.py:457
  60.3 1.6 %shard_map.94 = (bf16[512,1280]{1,0:T(8,128)(2,1)}, f32[5,8]{1,0:T(8,128)}, f32[320,640]{1,0:T(8,128)}, f32[320,640]{1,0:T(8,128)}) custom-call(bf16[512,1280]{1,0:T(8,128)(2,1)S(1)} %get-tuple-element.12.refs_0_, f32[5,8]{1,0:T(8,128)S(1)} %get-tuple-element.13.refs_1_, f32[320,640]{1,0:T(8,128)S(1)} %get-tuple-element.14.refs_2_, ...), custom_call_target="tpu_custom_call" | custom-call | tf_op jit(solution)/shard_map/pallas_call | solution.py:515
